TPU v7x, 512 devices: a whole 4x4x16 slice. The times are simulated.
512 devices in a mesh: dp: 64 (over z, x), tensor: 8 (over y, core).
Axes of the slice: x: 4, y: 4, z: 16, core: 2. Of those that a mesh axis runs over, the one named last changes fastest.
Arguments:
- gradient: float32 [64, 512, 4096], P('dp', 'tensor'), may hold values from -90 to 90
- error_buffer: float32 [64, 512, 4096], P('dp', 'tensor'), may hold values from -6 to 6
- right_factor: float32 [4096, 32], replicated, may hold values from -6 to 6
Outputs:
- averaged: float32 [512, 4096], P('tensor')
- new_error: float32 [64, 512, 4096], P('dp', 'tensor')
All inputs are finite; a program needn't handle non-finite values.
Results may differ from a plain program's by a relative error of at most 0.0003.
Values sent between devices are 32-bit elements; how exact they have to be, the bound alone decides.
No kernel may reach another device: no remote copies, remote signals or barrier semaphores. Data moves between devices by JAX's collectives and lax.ppermute only.
A program may use at most 64 MiB of HBM per device.

v0:
```python
import jax
import jax.numpy as jnp
from jax import lax
from jax.sharding import PartitionSpec as P


def shards(gradient, error_buffer, right_factor):
    highest = lax.Precision.HIGHEST
    corrected = gradient[0] + error_buffer[0]
    local_left = jnp.dot(corrected, right_factor, precision=highest)
    left_sum = lax.psum(local_left, "dp")
    gram = lax.psum(jnp.dot(left_sum.T, left_sum, precision=highest), "tensor")
    lower = jnp.linalg.cholesky(gram)
    basis = lax.linalg.triangular_solve(
        lower, left_sum, left_side=False, lower=True, transpose_a=True
    )
    local_right = lax.dot_general(corrected, basis, (((0,), (0,)), ((), ())), precision=highest)
    replicas = lax.axis_size("dp")
    new_right = lax.psum(local_right, ("dp", "tensor")) / replicas
    averaged = lax.dot_general(basis, new_right, (((1,), (1,)), ((), ())), precision=highest)
    new_error = (corrected - averaged)[None]
    return (averaged, new_error)


def solution(mesh):
    in_specs = (P("dp", "tensor", None), P("dp", "tensor", None), P())
    out_specs = (P("tensor", None), P("dp", "tensor", None))
    return jax.shard_map(shards, mesh=mesh, in_specs=in_specs, out_specs=out_specs, check_vma=False)
```

profile of v0, /device:TPU:1, one launch (start us, length us, event | category | flops | bytes accessed | tf_op | source)
XLA Modules:
  0.0 787.7 jit_solution(12751642810058689909)
XLA Ops:
  7.2 0.0 copy-start
  7.2 0.0 copy-start.2
  7.2 0.0 copy-start.1
  7.2 0.0 all-reduce.2.cloned.1.call-start
  7.2 1.0 copy-done
  8.2 2.5 fusion.2
  10.7 231.3 %psum.21 = f32[64,32]{0,1:T(8,128)S(1)} all-reduce(f32[64,32]{0,1:T(8,128)S(1)} %fusion.2), channel_id=1, replica_groups=mesh['dp'=64,'tensor'=8] {'dp'}, use_global_device_ids=true, to_apply=%region_0.0 | all-reduce | flops 2048 | bytes 16384 | tf_op jit(solution)/shard_map/psum | solution.py:11
  242.0 0.1 fusion.15
  242.2 75.9 %psum.22 = f32[32,32]{0,1:T(8,128)S(1)} all-reduce(f32[32,32]{0,1:T(8,128)S(1)} %fusion.15), channel_id=1, replica_groups=mesh['dp'=64,'tensor'=8] {'tensor'}, use_global_device_ids=true, to_apply=%region_1.0 | all-reduce | flops 1024 | bytes 8192 | tf_op jit(solution)/shard_map/psum | solution.py:12
  318.1 0.1 copy.8
  318.2 2.9 cholesky.16
  321.1 0.6 compare_reduce_fusion
  321.8 0.7 fusion.8
  322.4 2.4 custom-call.6
  324.8 0.2 fusion.9
  325.1 0.0 copy-done.2
  325.1 0.0 copy-done.1
  325.1 1.5 fusion
  326.6 0.0 all-reduce.2.cloned.1.call-update
  326.7 450.8 %all-reduce.2.cloned.1.call-done = f32[4096,32]{0,1:T(8,128)} async-done(((f32[4096,32]{0,1:T(8,128)}), f32[4096,32]{0,1:T(8,128)}) %all-reduce.2.cloned.1.call-update) | async-done | bytes 524304 | tf_op jit(solution)/shard_map/psum | solution.py:19
  777.5 2.1 fusion.5
  779.6 0.0 copy-start.3
  779.6 1.3 fusion.4
  780.9 0.0 copy-done.3
  (2 shorter events, 0.0 us)
Async XLA Ops:
  7.2 1.0 copy-start
  7.2 317.9 %copy-start.2 = (f32[1,64,4096]{2,1,0:T(8,128)S(1)}, f32[1,64,4096]{2,1,0:T(8,128)}, u32[]{:S(2)}) copy-start(f32[1,64,4096]{2,1,0:T(8,128)} %param.4) | copy-start | bytes 3145732
  7.2 317.9 %copy-start.1 = (f32[1,64,4096]{2,1,0:T(8,128)S(1)}, f32[1,64,4096]{2,1,0:T(8,128)}, u32[]{:S(2)}) copy-start(f32[1,64,4096]{2,1,0:T(8,128)} %param.3) | copy-start | bytes 3145732
  7.2 770.3 %all-reduce.2.cloned.1.call-start = ((), (), s32[]{:S(2)}) async-start(), calls=%async_computation | async-start | bytes 1048576 | tf_op jit(solution)/shard_map/psum | solution.py:19
  779.6 1.3 copy-start.3
Sparse Core Ops, SparseCore 0:
  326.8 450.6 all-reduce.1
where the time goes:
time: 789 us; the launch traced here: 788 us
  waiting for transfers between devices  451 us (57%)
  blocking collectives  307 us (39%)
  between operations  14.1 us (2%)
  other arithmetic  7.99 us (1%)
    psum x1, waiting for transfers between devices, shards(): new_right = lax.psum(local_right, ('dp', 'tensor')) / replicas  451 us
    psum x1, blocking collectives, shards(): left_sum = lax.psum(local_left, 'dp')  231 us
    psum x1, blocking collectives, shards(): gram = lax.psum(jnp.dot(left_sum.T, left_sum, precision=highest), 'tensor')  75.9 us
  transfers between devices with their start and end apart: 1, of which 1 were waited for; matrix products, arithmetic and copies ran while one was open for 0% of the time, Pallas kernels for 0%

commit v1 on v0

v1 whole, which is shorter than its diff:
```python
import jax
import jax.numpy as jnp
from jax import lax
from jax.sharding import Mesh, PartitionSpec as P

AXES = ("z", "x", "y", "core")


def copies(block, axis):
    count = lax.axis_size(axis)
    return lax.all_to_all(jnp.broadcast_to(block[None], (count,) + block.shape), axis, 0, 0)


def pack(matrix):
    rows = matrix.shape[0]
    return matrix.reshape(4, rows // 4, 32).transpose(1, 0, 2).reshape(rows // 4, 128)


def unpack(dense):
    rows = dense.shape[0]
    return dense.reshape(rows, 4, 32).transpose(1, 0, 2).reshape(rows * 4, 32)


def shards(gradient, error_buffer, right_factor):
    highest = lax.Precision.HIGHEST
    rank = right_factor.shape[1]
    width = right_factor.shape[0]
    corrected = gradient[0] + error_buffer[0]
    local_left = pack(jnp.dot(corrected, right_factor, precision=highest))
    left_sum = unpack(copies(copies(local_left, "x").sum(0), "z").sum(0))
    plane = ("x", "y", "core")
    peers = lax.axis_size(plane)
    share = width // peers
    part = lax.dot_general(left_sum, corrected, (((0,), (0,)), ((), ())), precision=highest)
    part = part.reshape(rank, peers, share).transpose(1, 0, 2)
    gram = pack(lax.dot_general(left_sum, left_sum, (((0,), (0,)), ((), ())), precision=highest))
    sent = jnp.concatenate([part, jnp.broadcast_to(gram[None], (peers,) + gram.shape)], axis=1)
    got = lax.all_to_all(sent, plane, 0, 0).sum(0)
    gram = unpack(got[rank:]) / lax.axis_size("x")
    mine = copies(got[:rank], "z").sum(0)
    whole = lax.all_gather(copies(mine, ("x", "y")), "core")
    whole = whole.transpose(2, 1, 0, 3).reshape(rank, width)
    lower = jnp.linalg.cholesky(gram)
    basis = lax.linalg.triangular_solve(
        lower, left_sum, left_side=False, lower=True, transpose_a=True
    )
    back = lax.linalg.triangular_solve(
        lower, basis, left_side=False, lower=True, transpose_a=False
    )
    replicas = lax.axis_size("z") * lax.axis_size("x")
    averaged = jnp.dot(back, whole, precision=highest) / replicas
    new_error = (corrected - averaged)[None]
    return (averaged, new_error)


def solution(mesh):
    fine = Mesh(mesh.devices.reshape(16, 4, 4, 2), AXES)
    in_specs = (P(("z", "x"), ("y", "core"), None), P(("z", "x"), ("y", "core"), None), P())
    out_specs = (P(("y", "core"), None), P(("z", "x"), ("y", "core"), None))
    return jax.shard_map(shards, mesh=fine, in_specs=in_specs, out_specs=out_specs, check_vma=False)
```

time: 789 us -> 104 us (0.13)
  waiting for transfers between devices: 451 us -> 15.7 us
  blocking collectives: 307 us -> 63.8 us
  between operations: 14.1 us -> 0.79 us
    psum x1 -> x0, waiting for transfers between devices: 451 us -> none  [shards(): new_right = lax.psum(local_right, ('dp', 'tensor')) / replicas]
    psum x2 -> x0, blocking collectives: 307 us -> none  [the longest x1 231 us: shards(): left_sum = lax.psum(local_left, 'dp')]
    all_to_all x0 -> x3, blocking collectives: none -> 57.9 us  [the longest x2 35.7 us: copies(): lax.all_to_all(jnp.broadcast_to(block[None], (count,) + block.shape), axi...]
    all_to_all x0 -> x2, waiting for transfers between devices: none -> 15.7 us  [copies(): lax.all_to_all(jnp.broadcast_to(block[None], (count,) + block.shape), axi...]
  transfers between devices with their start and end apart: 1 -> 2, of which waited for: 1 -> 2; matrix products, arithmetic and copies ran while one was open for 0% -> 7% of each run, Pallas kernels for 0% -> 0%
where the time goes in v1:
time: 104 us
  blocking collectives  63.8 us (61%)
  waiting for transfers between devices  15.7 us (15%)
  other arithmetic  9.74 us (9%)
  starting transfers between devices  7.45 us (7%)
  matrix products  3.13 us (3%)
  local copies, waits for them, and re-layouts  2.94 us (3%)
    all_to_all x2, blocking collectives, copies(): lax.all_to_all(jnp.broadcast_to(block[None], (count,) + block.shape), axi...  35.7 us
    all_to_all x1, blocking collectives, shards(): got = lax.all_to_all(sent, plane, 0, 0).sum(0)  22.3 us
    all_to_all x2, waiting for transfers between devices, copies(): lax.all_to_all(jnp.broadcast_to(block[None], (count,) + block.shape), axi...  15.7 us
    all_to_all x2, starting transfers between devices, copies(): lax.all_to_all(jnp.broadcast_to(block[None], (count,) + block.shape), axi...  7.45 us
    all_gather x1, blocking collectives, shards(): whole = lax.all_gather(copies(mine, ('x', 'y')), 'core')  5.85 us
    another operation x3, other arithmetic, shards(): lower = jnp.linalg.cholesky(gram)  3.6 us
    another operation x2, other arithmetic, shards(): lax.linalg.triangular_solve(lower, left_sum, left_side=False, lower=True,...  3.09 us
  transfers between devices with their start and end apart: 2, of which 2 were waited for; matrix products, arithmetic and copies ran while one was open for 7% of the time, Pallas kernels for 0%

profile of v1, /device:TPU:1, one launch (start us, length us, event | category | flops | bytes accessed | tf_op | source)
XLA Modules:
  0.0 103.5 jit_solution(9268689392357617442)
XLA Ops:
  0.6 1.7 %add.23 = f32[1,64,4096]{2,1,0:T(8,128)S(1)} add(f32[1,64,4096]{2,1,0:T(8,128)} %param.3, f32[1,64,4096]{2,1,0:T(8,128)} %param.4) | non-fusion elementwise | flops 262144 | bytes 3145728 | tf_op jit(solution)/shard_map/add | solution.py:28
  2.4 1.0 convolution_bitcast_fusion.1
  3.4 8.9 %all_to_all.25 = f32[4,16,128]{2,1,0:T(8,128)S(1)} all-to-all(f32[4,16,128]{2,1,0:T(8,128)S(1)} %broadcast_in_dim.18), channel_id=1, replica_groups=mesh['z'=16,'x'=4,'y'=4,'core'=2] {'x'}, dimensions={0} | all-to-all | bytes 65536 | tf_op jit(solution)/shard_map/all_to_all | solution.py:11
  12.4 26.7 %all_to_all.26 = f32[16,16,128]{2,1,0:T(8,128)S(1)} all-to-all(f32[16,16,128]{2,1,0:T(8,128)S(1)} %broadcast_in_dim.20), channel_id=1, replica_groups=mesh['z'=16,'x'=4,'y'=4,'core'=2] {'z'}, dimensions={0} | all-to-all | bytes 262144 | tf_op jit(solution)/shard_map/all_to_all | solution.py:11
  39.3 0.7 convolution_bitcast_fusion
  40.0 0.1 convolution_bitcast_fusion.2
  40.3 22.3 %all_to_all.27 = f32[32,40,128]{2,1,0:T(8,128)S(1)} all-to-all(f32[32,40,128]{2,1,0:T(8,128)S(1)} %pad_maximum_fusion), channel_id=1, replica_groups=mesh['z'=16,'x'=4,'y'=4,'core'=2] {'x','y','core'}, dimensions={0} | all-to-all | bytes 1310720 | tf_op jit(solution)/shard_map/all_to_all | solution.py:38
  62.6 0.7 broadcast_in_dim.42
  63.3 3.5 %all-to-all-start.3 = ((f32[16,32,128]{2,1,0:T(8,128)}), f32[16,32,128]{2,1,0:T(8,128)S(1)}, u32[]{:S(2)}, u32[]{:S(2)}) async-start(f32[16,32,128]{2,1,0:T(8,128)} %broadcast_in_dim.42), calls=%async_computation.3 | async-start | bytes 524288 | tf_op jit(solution)/shard_map/all_to_all | solution.py:11
  67.0 2.9 %cholesky.16 = f32[32,32]{1,0:T(8,128)S(1)} custom-call(f32[32,32]{1,0:T(8,128)S(1)} %fusion.9), custom_call_target="Cholesky" | custom-call | tf_op jit(solution)/shard_map/jit(cholesky)/cholesky | solution.py:43
  70.0 0.6 compare_reduce_fusion
  70.6 0.7 fusion.4
  71.3 2.4 %custom-call.8 = f32[1,32,32]{1,2,0:T(8,128)S(1)} custom-call(f32[1,32,32]{2,1,0:T(8,128)S(1)} %fusion.4), custom_call_target="InvertDiagBlocksLowerTriangular" | custom-call | tf_op jit(solution)/shard_map/triangular_solve | solution.py:44
  73.7 8.7 %all-to-all-done.3 = f32[16,32,128]{2,1,0:T(8,128)S(1)} async-done(((f32[16,32,128]{2,1,0:T(8,128)}), f32[16,32,128]{2,1,0:T(8,128)S(1)}, u32[]{:S(2)}, u32[]{:S(2)}) %all-to-all-start.3) | async-done | bytes 262176 | tf_op jit(solution)/shard_map/all_to_all | solution.py:11
  82.5 0.7 broadcast_in_dim.43
  83.2 3.9 %all-to-all-start.4 = ((f32[16,32,128]{2,1,0:T(8,128)}), f32[16,32,128]{2,1,0:T(8,128)S(1)}, u32[]{:S(2)}, u32[]{:S(2)}) async-start(f32[16,32,128]{2,1,0:T(8,128)} %broadcast_in_dim.43), calls=%async_computation.4 | async-start | bytes 524288 | tf_op jit(solution)/shard_map/all_to_all | solution.py:11
  87.2 0.2 fusion.7
  87.4 0.1 fusion.5
  87.5 7.0 %all-to-all-done.4 = f32[16,32,128]{2,1,0:T(8,128)S(1)} async-done(((f32[16,32,128]{2,1,0:T(8,128)}), f32[16,32,128]{2,1,0:T(8,128)S(1)}, u32[]{:S(2)}, u32[]{:S(2)}) %all-to-all-start.4) | async-done | bytes 262176 | tf_op jit(solution)/shard_map/all_to_all | solution.py:11
  94.5 5.8 %all-gather = f32[32,32,128]{2,1,0:T(8,128)S(1)} all-gather(f32[16,32,128]{2,1,0:T(8,128)S(1)} %all-to-all-done.4), channel_id=2, replica_groups=mesh['z'=16,'x'=4,'y'=4,'core'=2] {'core'}, dimensions={0}, use_global_device_ids=true | all-gather | bytes 786432 | tf_op jit(solution)/shard_map/all_gather | solution.py:41
  100.3 0.4 copy.45
  100.8 0.4 reshape.47
  101.2 1.0 convolution_multiply_fusion
  102.2 1.2 %fusion.2 = f32[1,64,4096]{2,1,0:T(8,128)} fusion(f32[64,4096]{1,0:T(8,128)S(1)} %convolution_multiply_fusion, f32[1,64,4096]{2,1,0:T(8,128)S(1)} %add.23), kind=kLoop, calls=%fused_computation.7 | loop fusion | flops 262144 | bytes 3145728 | tf_op jit(solution)/shard_map/broadcast_in_dim | solution.py:52
  (26 shorter events, 0.8 us)
Async XLA Ops:
  0.6 1.7 %copy-start = (f32[4096,32]{0,1:T(8,128)S(1)}, f32[4096,32]{0,1:T(8,128)}, u32[]{:S(2)}) copy-start(f32[4096,32]{0,1:T(8,128)} %param.5) | copy-start | bytes 1572868
  63.3 19.1 %all-to-all-start.3 = ((f32[16,32,128]{2,1,0:T(8,128)}), f32[16,32,128]{2,1,0:T(8,128)S(1)}, u32[]{:S(2)}, u32[]{:S(2)}) async-start(f32[16,32,128]{2,1,0:T(8,128)} %broadcast_in_dim.42), calls=%async_computation.3 | async-start | bytes 524288 | tf_op jit(solution)/shard_map/all_to_all | solution.py:11
  83.2 11.3 %all-to-all-start.4 = ((f32[16,32,128]{2,1,0:T(8,128)}), f32[16,32,128]{2,1,0:T(8,128)S(1)}, u32[]{:S(2)}, u32[]{:S(2)}) async-start(f32[16,32,128]{2,1,0:T(8,128)} %broadcast_in_dim.43), calls=%async_computation.4 | async-start | bytes 524288 | tf_op jit(solution)/shard_map/all_to_all | solution.py:11
  102.2 1.3 %copy-start.1 = (f32[64,4096]{1,0:T(8,128)}, f32[64,4096]{1,0:T(8,128)S(1)}, u32[]{:S(2)}) copy-start(f32[64,4096]{1,0:T(8,128)S(1)} %convolution_multiply_fusion) | copy-start | bytes 3145732

commit v2 on v1

v2 whole, which is shorter than its diff:
```python
import jax
import jax.numpy as jnp
from jax import lax
from jax.sharding import Mesh, PartitionSpec as P

AXES = ("far", "near", "x", "y", "core")
DP = ("far", "near", "x")
TENSOR = ("y", "core")
HIGHEST = lax.Precision.HIGHEST


def copies(block, axis):
    count = lax.axis_size(axis)
    return lax.all_to_all(jnp.broadcast_to(block[None], (count,) + block.shape), axis, 0, 0)


def pack(matrix):
    rows = matrix.shape[0]
    return matrix.reshape(4, rows // 4, 32).transpose(1, 0, 2).reshape(rows // 4, 128)


def unpack(dense):
    rows = dense.shape[0]
    return dense.reshape(rows, 4, 32).transpose(1, 0, 2).reshape(rows * 4, 32)


def shards(gradient, error_buffer, right_factor):
    width, rank = right_factor.shape
    columns, near, tensor = lax.axis_size("x"), lax.axis_size("near"), lax.axis_size(TENSOR)
    span = width // columns
    share = span // tensor
    half = rank // near
    corrected = gradient[0] + error_buffer[0]
    local_left = pack(jnp.dot(corrected, right_factor, precision=HIGHEST))
    left_sum = unpack(copies(copies(local_left, "x").sum(0), ("far", "near")).sum(0))

    here = lax.axis_index("x")

    def block(at):
        return lax.dynamic_slice_in_dim(corrected, lax.rem(here + at, columns) * span, span, axis=1)

    moved = block(0)
    for step in range(1, columns):
        ring = [(i, (i + step) % columns) for i in range(columns)]
        moved = moved + lax.ppermute(block(step), "x", ring)

    part = lax.dot_general(left_sum, moved, (((0,), (0,)), ((), ())), precision=HIGHEST)
    part = part.reshape(near, half, tensor, share).transpose(0, 2, 1, 3).reshape(near * tensor, half, share)
    gram = pack(lax.dot_general(left_sum, left_sum, (((0,), (0,)), ((), ())), precision=HIGHEST))
    sent = jnp.concatenate([part, jnp.broadcast_to(gram[None], (near * tensor,) + gram.shape)], axis=1)
    got = lax.all_to_all(sent, ("near",) + TENSOR, 0, 0).sum(0)
    gram = unpack(got[half:]) / near
    mine = copies(got[:half], "far").sum(0)
    whole = lax.all_gather(copies(mine, ("near", "x", "y")), "core")
    whole = whole.reshape(2, near, columns, tensor // 2, half, share).transpose(1, 4, 2, 3, 0, 5)
    whole = whole.reshape(rank, width)

    lower = jnp.linalg.cholesky(gram)
    basis = lax.linalg.triangular_solve(
        lower, left_sum, left_side=False, lower=True, transpose_a=True
    )
    back = lax.linalg.triangular_solve(
        lower, basis, left_side=False, lower=True, transpose_a=False
    )
    averaged = jnp.dot(back, whole, precision=HIGHEST) / lax.axis_size(DP)
    new_error = (corrected - averaged)[None]
    return (averaged, new_error)


def solution(mesh):
    fine = Mesh(mesh.devices.reshape(8, 2, 4, 4, 2), AXES)
    in_specs = (P(DP, TENSOR, None), P(DP, TENSOR, None), P())
    out_specs = (P(TENSOR, None), P(DP, TENSOR, None))
    return jax.shard_map(shards, mesh=fine, in_specs=in_specs, out_specs=out_specs, check_vma=False)
```

time: 104 us -> 106 us (1.019)
  blocking collectives: 63.8 us -> 30.9 us
  starting transfers between devices: 7.45 us -> 38.9 us
  waiting for transfers between devices: 15.7 us -> 19.2 us
    all_to_all x2 -> x1, blocking collectives: 35.7 us -> 8.93 us  [copies(): lax.all_to_all(jnp.broadcast_to(block[None], (count,) + block.shape), axi...]
    all_to_all x2 -> x3, starting transfers between devices: 7.45 us -> 30.4 us  [copies(): lax.all_to_all(jnp.broadcast_to(block[None], (count,) + block.shape), axi...]
    ppermute x0 -> x3, starting transfers between devices: none -> 8.41 us  [shards(): moved = moved + lax.ppermute(block(step), 'x', ring)]
    all_to_all x1, blocking collectives: 22.3 us -> 16.2 us  [shards(): got = lax.all_to_all(sent, ('near',) + TENSOR, 0, 0).sum(0)]
    ppermute x0 -> x3, waiting for transfers between devices: none -> 2.99 us  [shards(): moved = moved + lax.ppermute(block(step), 'x', ring)]
    all_to_all x2 -> x3, waiting for transfers between devices: 15.7 us -> 16.2 us  [copies(): lax.all_to_all(jnp.broadcast_to(block[None], (count,) + block.shape), axi...]
  transfers between devices with their start and end apart: 2 -> 6, of which waited for: 2 -> 4; matrix products, arithmetic and copies ran while one was open for 7% -> 7% of each run, Pallas kernels for 0% -> 0%
where the time goes in v2:
time: 106 us
  starting transfers between devices  38.9 us (37%)
  blocking collectives  30.9 us (29%)
  waiting for transfers between devices  19.2 us (18%)
  other arithmetic  9.66 us (9%)
  local copies, waits for them, and re-layouts  3.57 us (3%)
  matrix products  2.8 us (3%)
    all_to_all x3, starting transfers between devices, copies(): lax.all_to_all(jnp.broadcast_to(block[None], (count,) + block.shape), axi...  30.4 us
    all_to_all x3, waiting for transfers between devices, copies(): lax.all_to_all(jnp.broadcast_to(block[None], (count,) + block.shape), axi...  16.2 us
    all_to_all x1, blocking collectives, shards(): got = lax.all_to_all(sent, ('near',) + TENSOR, 0, 0).sum(0)  16.2 us
    all_to_all x1, blocking collectives, copies(): lax.all_to_all(jnp.broadcast_to(block[None], (count,) + block.shape), axi...  8.93 us
    ppermute x3, starting transfers between devices, shards(): moved = moved + lax.ppermute(block(step), 'x', ring)  8.41 us
    all_gather x1, blocking collectives, shards(): whole = lax.all_gather(copies(mine, ('near', 'x', 'y')), 'core')  5.75 us
    another operation x3, other arithmetic, shards(): lower = jnp.linalg.cholesky(gram)  3.59 us
    another operation x2, other arithmetic, shards(): lax.linalg.triangular_solve(lower, left_sum, left_side=False, lower=True,...  3.09 us
  transfers between devices with their start and end apart: 6, of which 4 were waited for; matrix products, arithmetic and copies ran while one was open for 7% of the time, Pallas kernels for 0%

profile of v2, /device:TPU:1, one launch (start us, length us, event | category | flops | bytes accessed | tf_op | source)
XLA Modules:
  0.0 105.9 jit_solution(13761068207945637507)
XLA Ops:
  0.6 1.7 %add.53 = f32[1,64,4096]{2,1,0:T(8,128)S(1)} add(f32[1,64,4096]{2,1,0:T(8,128)} %param.3, f32[1,64,4096]{2,1,0:T(8,128)} %param.4) | non-fusion elementwise | flops 262144 | bytes 3145728 | tf_op jit(solution)/shard_map/add | solution.py:33
  2.4 1.0 convolution_bitcast_fusion
  3.4 8.9 %all_to_all.25 = f32[4,16,128]{2,1,0:T(8,128)S(1)} all-to-all(f32[4,16,128]{2,1,0:T(8,128)S(1)} %broadcast_in_dim.18), channel_id=1, replica_groups=mesh['far'=8,'near'=2,'x'=4,'y'=4,'core'=2] {'x'}, dimensions={0} | all-to-all | bytes 65536 | tf_op jit(solution)/shard_map/all_to_all | solution.py:14
  12.4 0.7 broadcast_in_dim.20
  13.1 14.9 %all-to-all-start.1 = ((f32[16,16,128]{2,1,0:T(8,128)}), f32[16,16,128]{2,1,0:T(8,128)S(1)}, u32[]{:S(2)}, u32[]{:S(2)}) async-start(f32[16,16,128]{2,1,0:T(8,128)} %broadcast_in_dim.20), calls=%async_computation.1 | async-start | bytes 262144 | tf_op jit(solution)/shard_map/all_to_all | solution.py:14
  28.1 2.2 %collective-permute-start = (f32[64,1024]{1,0:T(8,128)S(1)}, f32[64,1024]{1,0:T(8,128)S(1)}, u32[]{:S(2)}, u32[]{:S(2)}) collective-permute-start(f32[64,1024]{1,0:T(8,128)S(1)} %get-tuple-element.2), channel_id=1, source_target_pairs={{0,8},{8,16},{16,24},{24,0},{1,9},{9,17},{17,25},{25,1},{2,10},{10... | collective-permute-start | bytes 786440 | tf_op jit(solution)/shard_map/ppermute | solution.py:45
  30.3 4.3 %collective-permute-start.2 = (f32[64,1024]{1,0:T(8,128)S(1)}, f32[64,1024]{1,0:T(8,128)S(1)}, u32[]{:S(2)}, u32[]{:S(2)}) collective-permute-start(f32[64,1024]{1,0:T(8,128)S(1)} %get-tuple-element.3), channel_id=1, source_target_pairs={{0,24},{8,0},{16,8},{24,16},{1,25},{9,1},{17,9},{25,17},{2,26},{10... | collective-permute-start | bytes 786440 | tf_op jit(solution)/shard_map/ppermute | solution.py:45
  34.6 1.9 %collective-permute-start.1 = (f32[64,1024]{1,0:T(8,128)S(1)}, f32[64,1024]{1,0:T(8,128)S(1)}, u32[]{:S(2)}, u32[]{:S(2)}) collective-permute-start(f32[64,1024]{1,0:T(8,128)S(1)} %get-tuple-element.4), channel_id=1, source_target_pairs={{0,16},{8,24},{16,0},{24,8},{1,17},{9,25},{17,1},{25,9},{2,18},{10... | collective-permute-start | bytes 786440 | tf_op jit(solution)/shard_map/ppermute | solution.py:45
  36.5 3.5 %all-to-all-done.1 = f32[16,16,128]{2,1,0:T(8,128)S(1)} async-done(((f32[16,16,128]{2,1,0:T(8,128)}), f32[16,16,128]{2,1,0:T(8,128)S(1)}, u32[]{:S(2)}, u32[]{:S(2)}) %all-to-all-start.1) | async-done | bytes 131104 | tf_op jit(solution)/shard_map/all_to_all | solution.py:14
  40.4 3.0 %collective-permute-done.1 = f32[64,1024]{1,0:T(8,128)S(1)} collective-permute-done((f32[64,1024]{1,0:T(8,128)S(1)}, f32[64,1024]{1,0:T(8,128)S(1)}, u32[]{:S(2)}, u32[]{:S(2)}) %collective-permute-start.1) | collective-permute-done | bytes 262176 | tf_op jit(solution)/shard_map/ppermute | solution.py:45
  43.7 16.2 %all_to_all.26 = f32[16,24,128]{2,1,0:T(8,128)S(1)} all-to-all(f32[16,24,128]{2,1,0:T(8,128)S(1)} %pad_maximum_fusion), channel_id=1, replica_groups=mesh['far'=8,'near'=2,'x'=4,'y'=4,'core'=2] {'near','y','core'}, dimensions={0} | all-to-all | bytes 393216 | tf_op jit(solution)/shard_map/all_to_all | solution.py:51
  60.0 0.6 broadcast_in_dim.42
  60.6 10.3 %all-to-all-start.3 = ((f32[8,16,128]{2,1,0:T(8,128)}), f32[8,16,128]{2,1,0:T(8,128)S(1)}, u32[]{:S(2)}, u32[]{:S(2)}) async-start(f32[8,16,128]{2,1,0:T(8,128)} %broadcast_in_dim.42), calls=%async_computation.3 | async-start | bytes 131072 | tf_op jit(solution)/shard_map/all_to_all | solution.py:14
  71.0 11.9 %all-to-all-done.3 = f32[8,16,128]{2,1,0:T(8,128)S(1)} async-done(((f32[8,16,128]{2,1,0:T(8,128)}), f32[8,16,128]{2,1,0:T(8,128)S(1)}, u32[]{:S(2)}, u32[]{:S(2)}) %all-to-all-start.3) | async-done | bytes 65568 | tf_op jit(solution)/shard_map/all_to_all | solution.py:14
  82.9 0.7 broadcast_in_dim.43
  83.6 5.3 %all-to-all-start.4 = ((f32[32,16,128]{2,1,0:T(8,128)}), f32[32,16,128]{2,1,0:T(8,128)S(1)}, u32[]{:S(2)}, u32[]{:S(2)}) async-start(f32[32,16,128]{2,1,0:T(8,128)} %broadcast_in_dim.43), calls=%async_computation.4 | async-start | bytes 524288 | tf_op jit(solution)/shard_map/all_to_all | solution.py:14
  88.9 2.9 %cholesky.16 = f32[32,32]{1,0:T(8,128)S(1)} custom-call(f32[32,32]{1,0:T(8,128)S(1)} %fusion.12), custom_call_target="Cholesky" | custom-call | tf_op jit(solution)/shard_map/jit(cholesky)/cholesky | solution.py:58
  91.9 0.6 compare_reduce_fusion
  92.5 0.7 fusion.7
  93.2 2.4 %custom-call.8 = f32[1,32,32]{1,2,0:T(8,128)S(1)} custom-call(f32[1,32,32]{2,1,0:T(8,128)S(1)} %fusion.7), custom_call_target="InvertDiagBlocksLowerTriangular" | custom-call | tf_op jit(solution)/shard_map/triangular_solve | solution.py:59
  96.0 0.9 all-to-all-done.4
  96.9 5.7 %all-gather = f32[64,16,128]{2,1,0:T(8,128)S(1)} all-gather(f32[32,16,128]{2,1,0:T(8,128)S(1)} %all-to-all-done.4), channel_id=2, replica_groups=mesh['far'=8,'near'=2,'x'=4,'y'=4,'core'=2] {'core'}, dimensions={0}, use_global_device_ids=true | all-gather | bytes 786432 | tf_op jit(solution)/shard_map/all_gather | solution.py:54
  103.5 1.0 convolution_multiply_fusion
  104.5 1.2 %fusion = f32[1,64,4096]{2,1,0:T(8,128)} fusion(f32[64,4096]{1,0:T(8,128)S(1)} %convolution_multiply_fusion, f32[1,64,4096]{2,1,0:T(8,128)S(1)} %add.53), kind=kLoop, calls=%fused_computation.4 | loop fusion | flops 262144 | bytes 3145728 | tf_op jit(solution)/shard_map/broadcast_in_dim | solution.py:66
  (34 shorter events, 2.5 us)
Async XLA Ops:
  0.6 1.7 %copy-start = (f32[4096,32]{0,1:T(8,128)S(1)}, f32[4096,32]{0,1:T(8,128)}, u32[]{:S(2)}) copy-start(f32[4096,32]{0,1:T(8,128)} %param.5) | copy-start | bytes 1572868
  13.1 26.9 %all-to-all-start.1 = ((f32[16,16,128]{2,1,0:T(8,128)}), f32[16,16,128]{2,1,0:T(8,128)S(1)}, u32[]{:S(2)}, u32[]{:S(2)}) async-start(f32[16,16,128]{2,1,0:T(8,128)} %broadcast_in_dim.20), calls=%async_computation.1 | async-start | bytes 262144 | tf_op jit(solution)/shard_map/all_to_all | solution.py:14
  28.1 12.3 %collective-permute-start = (f32[64,1024]{1,0:T(8,128)S(1)}, f32[64,1024]{1,0:T(8,128)S(1)}, u32[]{:S(2)}, u32[]{:S(2)}) collective-permute-start(f32[64,1024]{1,0:T(8,128)S(1)} %get-tuple-element.2), channel_id=1, source_target_pairs={{0,8},{8,16},{16,24},{24,0},{1,9},{9,17},{17,25},{25,1},{2,10},{10... | collective-permute-start | bytes 786440 | tf_op jit(solution)/shard_map/ppermute | solution.py:45
  30.3 10.1 %collective-permute-start.2 = (f32[64,1024]{1,0:T(8,128)S(1)}, f32[64,1024]{1,0:T(8,128)S(1)}, u32[]{:S(2)}, u32[]{:S(2)}) collective-permute-start(f32[64,1024]{1,0:T(8,128)S(1)} %get-tuple-element.3), channel_id=1, source_target_pairs={{0,24},{8,0},{16,8},{24,16},{1,25},{9,1},{17,9},{25,17},{2,26},{10... | collective-permute-start | bytes 786440 | tf_op jit(solution)/shard_map/ppermute | solution.py:45
  34.6 8.8 %collective-permute-start.1 = (f32[64,1024]{1,0:T(8,128)S(1)}, f32[64,1024]{1,0:T(8,128)S(1)}, u32[]{:S(2)}, u32[]{:S(2)}) collective-permute-start(f32[64,1024]{1,0:T(8,128)S(1)} %get-tuple-element.4), channel_id=1, source_target_pairs={{0,16},{8,24},{16,0},{24,8},{1,17},{9,25},{17,1},{25,9},{2,18},{10... | collective-permute-start | bytes 786440 | tf_op jit(solution)/shard_map/ppermute | solution.py:45
  60.6 22.3 %all-to-all-start.3 = ((f32[8,16,128]{2,1,0:T(8,128)}), f32[8,16,128]{2,1,0:T(8,128)S(1)}, u32[]{:S(2)}, u32[]{:S(2)}) async-start(f32[8,16,128]{2,1,0:T(8,128)} %broadcast_in_dim.42), calls=%async_computation.3 | async-start | bytes 131072 | tf_op jit(solution)/shard_map/all_to_all | solution.py:14
  83.6 13.3 %all-to-all-start.4 = ((f32[32,16,128]{2,1,0:T(8,128)}), f32[32,16,128]{2,1,0:T(8,128)S(1)}, u32[]{:S(2)}, u32[]{:S(2)}) async-start(f32[32,16,128]{2,1,0:T(8,128)} %broadcast_in_dim.43), calls=%async_computation.4 | async-start | bytes 524288 | tf_op jit(solution)/shard_map/all_to_all | solution.py:14
  104.5 1.3 %copy-start.1 = (f32[64,4096]{1,0:T(8,128)}, f32[64,4096]{1,0:T(8,128)S(1)}, u32[]{:S(2)}) copy-start(f32[64,4096]{1,0:T(8,128)S(1)} %convolution_multiply_fusion) | copy-start | bytes 3145732

commit v3 on v2

v3 whole, which is shorter than its diff:
```python
import jax
import jax.numpy as jnp
from jax import lax
from jax.experimental import pallas as pl
from jax.experimental.pallas import tpu as pltpu
from jax.sharding import Mesh, PartitionSpec as P

AXES = ("far", "near", "x", "y", "core")
DP = ("far", "near", "x")
TENSOR = ("y", "core")
CLOSE = ("near", "x")
HIGHEST = lax.Precision.HIGHEST
LANES = 128
VMEM_LIMIT = 16 * 2**20


def copies(block, axis):
    count = lax.axis_size(axis)
    return lax.all_to_all(jnp.broadcast_to(block[None], (count,) + block.shape), axis, 0, 0)


def pack(matrix):
    rows = matrix.shape[0]
    return matrix.reshape(4, rows // 4, 32).transpose(1, 0, 2).reshape(rows // 4, 128)


def unpack(dense):
    rows = dense.shape[0]
    return dense.reshape(rows, 4, 32).transpose(1, 0, 2).reshape(rows * 4, 32)


def beside(blocks, small):
    return jnp.concatenate([blocks, jnp.broadcast_to(small[None], blocks.shape[:1] + small.shape)], axis=1)


def first_kernel(gradient_ref, error_ref, right_ref, sent_ref, left_ref):
    step = pl.program_id(0)
    rows, span = gradient_ref.shape[1:]
    rank = right_ref.shape[0]
    corrected = gradient_ref[0] + error_ref[0]
    for tile in range(span // LANES):
        sent_ref[step, tile * rows : (tile + 1) * rows, :] = corrected[:, tile * LANES : (tile + 1) * LANES]
    part = lax.dot_general(
        corrected, right_ref[...], (((1,), (1,)), ((), ())), precision=HIGHEST, preferred_element_type=jnp.float32
    )

    @pl.when(step == 0)
    def _():
        left_ref[...] = part

    @pl.when(step > 0)
    def _():
        left_ref[...] += part

    @pl.when(step == pl.num_programs(0) - 1)
    def _():
        groups = LANES // rank
        high = rows // groups
        dense = jnp.concatenate([left_ref[g * high : (g + 1) * high, :] for g in range(groups)], axis=1)
        for block in range(sent_ref.shape[0]):
            sent_ref[block, span // LANES * rows :, :] = dense


def first(gradient, error_buffer, right, blocks):
    rank, width = right.shape
    rows = gradient.shape[1]
    span = width // blocks
    height = rows * span // LANES + rows * rank // LANES
    return pl.pallas_call(
        first_kernel,
        grid=(blocks,),
        in_specs=[
            pl.BlockSpec((1, rows, span), lambda i: (0, 0, i)),
            pl.BlockSpec((1, rows, span), lambda i: (0, 0, i)),
            pl.BlockSpec((rank, span), lambda i: (0, i)),
        ],
        out_specs=pl.BlockSpec((blocks, height, LANES), lambda i: (0, 0, 0)),
        out_shape=jax.ShapeDtypeStruct((blocks, height, LANES), jnp.float32),
        scratch_shapes=[pltpu.VMEM((rows, rank), jnp.float32)],
        compiler_params=pltpu.CompilerParams(vmem_limit_bytes=VMEM_LIMIT),
    )(gradient, error_buffer, right)


def last_kernel(back_ref, whole_ref, sent_ref, averaged_ref, error_ref):
    rows = back_ref.shape[0]
    low = lax.broadcasted_iota(jnp.int32, whole_ref.shape[2:], 1) < LANES // 2
    for block in range(whole_ref.shape[0]):
        upper, lower = [], []
        for pair in range(whole_ref.shape[1] // 2):
            even, odd = whole_ref[block, 2 * pair], whole_ref[block, 2 * pair + 1]
            upper.append(jnp.where(low, even, pltpu.roll(odd, LANES // 2, 1)))
            lower.append(jnp.where(low, pltpu.roll(even, LANES // 2, 1), odd))
        right = jnp.concatenate([jnp.concatenate(upper, axis=1), jnp.concatenate(lower, axis=1)], axis=0)
        averaged = jnp.dot(back_ref[...], right, precision=HIGHEST, preferred_element_type=jnp.float32)
        span = averaged.shape[1]
        averaged_ref[:, block * span : (block + 1) * span] = averaged
        for tile in range(span // LANES):
            columns = slice(block * span + tile * LANES, block * span + (tile + 1) * LANES)
            error_ref[0, :, columns] = (
                sent_ref[block, tile * rows : (tile + 1) * rows, :] - averaged[:, tile * LANES : (tile + 1) * LANES]
            )


def last(back, whole, sent, steps):
    rows, rank = back.shape
    blocks, height = sent.shape[0], sent.shape[1]
    each = blocks // steps
    span = whole.shape[1] * LANES // 2
    return pl.pallas_call(
        last_kernel,
        grid=(steps,),
        in_specs=[
            pl.BlockSpec((rows, rank), lambda i: (0, 0)),
            pl.BlockSpec((each,) + whole.shape[1:], lambda i: (i, 0, 0, 0)),
            pl.BlockSpec((each, height, LANES), lambda i: (i, 0, 0)),
        ],
        out_specs=[
            pl.BlockSpec((rows, each * span), lambda i: (0, i)),
            pl.BlockSpec((1, rows, each * span), lambda i: (0, 0, i)),
        ],
        out_shape=[
            jax.ShapeDtypeStruct((rows, blocks * span), jnp.float32),
            jax.ShapeDtypeStruct((1, rows, blocks * span), jnp.float32),
        ],
        compiler_params=pltpu.CompilerParams(vmem_limit_bytes=VMEM_LIMIT),
    )(back, whole, sent)


def shards(gradient, error_buffer, right_factor):
    width, rank = right_factor.shape
    rows = gradient.shape[1]
    close, far = lax.axis_size(CLOSE), lax.axis_size("far")
    tiles = width // close // LANES

    sent = first(gradient, error_buffer, right_factor.T, close)
    got = lax.all_to_all(sent, CLOSE, 0, 0).sum(0)
    blocks = got[: tiles * rows].reshape(tiles, 2, rows // 2, 2, LANES // 2).transpose(0, 3, 2, 1, 4)
    blocks = blocks.reshape(far, rows // 2, LANES)
    got = lax.all_to_all(beside(blocks, got[tiles * rows :]), "far", 0, 0).sum(0)
    left_sum = unpack(got[rows // 2 :])
    own = jnp.concatenate([got[: rows // 2, : LANES // 2], got[: rows // 2, LANES // 2 :]], axis=0)

    part = lax.dot_general(left_sum, own, (((0,), (0,)), ((), ())), precision=HIGHEST)
    part = jnp.concatenate([part[: rank // 2], part[rank // 2 :]], axis=1)
    gram = pack(lax.dot_general(left_sum, left_sum, (((0,), (0,)), ((), ())), precision=HIGHEST))
    got = copies(jnp.concatenate([part, gram], axis=0), TENSOR).sum(0)
    gram = unpack(got[rank // 2 :])
    whole = copies(got[: rank // 2], "far")

    lower = jnp.linalg.cholesky(gram)
    basis = lax.linalg.triangular_solve(
        lower, left_sum, left_side=False, lower=True, transpose_a=True
    )
    back = lax.linalg.triangular_solve(
        lower, basis, left_side=False, lower=True, transpose_a=False
    ) / lax.axis_size(DP)
    whole, back = lax.optimization_barrier((whole, back))
    whole = copies(whole, CLOSE)
    averaged, new_error = last(back, whole, sent, 4)
    return (averaged, new_error)


def solution(mesh):
    fine = Mesh(mesh.devices.reshape(8, 2, 4, 4, 2), AXES)
    in_specs = (P(DP, TENSOR, None), P(DP, TENSOR, None), P())
    out_specs = (P(TENSOR, None), P(DP, TENSOR, None))
    return jax.shard_map(shards, mesh=fine, in_specs=in_specs, out_specs=out_specs, check_vma=False)
```

time: 106 us -> 109 us (1.028)
  blocking collectives: 30.9 us -> 73.9 us
  starting transfers between devices: 38.9 us -> 3.35 us
  waiting for transfers between devices: 19.2 us -> 11.7 us
  Pallas kernels: 0 us -> 5.3 us
  other arithmetic: 9.66 us -> 6.87 us
  matrix products: 2.8 us -> 0.82 us
  local copies, waits for them, and re-layouts: 3.57 us -> 5.28 us
    all_to_all x1 -> x2, blocking collectives: 16.2 us -> 50.3 us  [the longest x1 31.2 us: shards(): got = lax.all_to_all(beside(blocks, got[tiles * rows:]), 'far', 0, 0).sum(0)]
    all_to_all x3 -> x1, starting transfers between devices: 30.4 us -> 3.35 us  [copies(): lax.all_to_all(jnp.broadcast_to(block[None], (count,) + block.shape), axi...]
    all_to_all x1 -> x2, blocking collectives: 8.93 us -> 23.6 us  [copies(): lax.all_to_all(jnp.broadcast_to(block[None], (count,) + block.shape), axi...]
    ppermute x3 -> x0, starting transfers between devices: 8.41 us -> none  [shards(): moved = moved + lax.ppermute(block(step), 'x', ring)]
    all_gather x1 -> x0, blocking collectives: 5.75 us -> none  [shards(): whole = lax.all_gather(copies(mine, ('near', 'x', 'y')), 'core')]
    pallas_call x0 -> x2, Pallas kernels: none -> 5.3 us  [the longest x1 2.87 us: last(): pl.pallas_call(last_kernel, grid=(steps,), in_specs=[pl.BlockSpec((rows,...]
    all_to_all x3 -> x1, waiting for transfers between devices: 16.2 us -> 11.7 us  [copies(): lax.all_to_all(jnp.broadcast_to(block[None], (count,) + block.shape), axi...]
    unnamed x4 -> x6, local copies, waits for them, and re-layouts: 0.12 us -> 3.48 us
  transfers between devices with their start and end apart: 6 -> 1, of which waited for: 4 -> 1; matrix products, arithmetic and copies ran while one was open for 7% -> 0% of each run, Pallas kernels for 0% -> 0%
where the time goes in v3:
time: 109 us; the launch traced here: 108 us
  blocking collectives  73.9 us (68%)
  waiting for transfers between devices  11.7 us (11%)
  other arithmetic  6.87 us (6%)
  Pallas kernels  5.3 us (5%)
  local copies, waits for them, and re-layouts  5.28 us (5%)
  starting transfers between devices  3.35 us (3%)
    all_to_all x1, blocking collectives, shards(): got = lax.all_to_all(beside(blocks, got[tiles * rows:]), 'far', 0, 0).sum(0)  31.2 us
    all_to_all x2, blocking collectives, copies(): lax.all_to_all(jnp.broadcast_to(block[None], (count,) + block.shape), axi...  23.6 us
    all_to_all x1, blocking collectives, shards(): got = lax.all_to_all(sent, CLOSE, 0, 0).sum(0)  19.1 us
    all_to_all x1, waiting for transfers between devices, copies(): lax.all_to_all(jnp.broadcast_to(block[None], (count,) + block.shape), axi...  11.7 us
    another operation x3, other arithmetic, shards(): lower = jnp.linalg.cholesky(gram)  3.6 us
    unnamed x6, local copies, waits for them, and re-layouts  3.48 us
    all_to_all x1, starting transfers between devices, copies(): lax.all_to_all(jnp.broadcast_to(block[None], (count,) + block.shape), axi...  3.35 us
    another operation x2, other arithmetic, shards(): lax.linalg.triangular_solve(lower, left_sum, left_side=False, lower=True,...  3.09 us
  transfers between devices with their start and end apart: 1, of which 1 were waited for; matrix products, arithmetic and copies ran while one was open for 0% of the time, Pallas kernels for 0%

profile of v3, /device:TPU:1, one launch (start us, length us, event | category | flops | bytes accessed | tf_op | source)
XLA Modules:
  0.0 108.0 jit_solution(15326532687094029099)
XLA Ops:
  0.6 1.2 %copy-done = f32[1,64,4096]{2,1,0:T(8,128)S(1)} copy-done((f32[1,64,4096]{2,1,0:T(8,128)S(1)}, f32[1,64,4096]{2,1,0:T(8,128)}, u32[]{:S(2)}) %copy-start) | copy-done | bytes 1048600
  1.9 1.2 %copy-done.1 = f32[1,64,4096]{2,1,0:T(8,128)S(1)} copy-done((f32[1,64,4096]{2,1,0:T(8,128)S(1)}, f32[1,64,4096]{2,1,0:T(8,128)}, u32[]{:S(2)}) %copy-start.1) | copy-done | bytes 1048600
  3.1 1.0 copy-done.2
  4.1 2.4 %shard_map.50.sent_ref = f32[8,272,128]{2,1,0:T(8,128)S(1)} custom-call(f32[1,64,4096]{2,1,0:T(8,128)S(1)} %copy-done, f32[1,64,4096]{2,1,0:T(8,128)S(1)} %copy-done.1, f32[32,4096]{1,0:T(8,128)S(1)} %bitcast.34), custom_call_target="tpu_custom_call" | custom-call | tf_op jit(solution)/shard_map/pallas_call | solution.py:69
  6.6 19.1 %all_to_all.25 = f32[8,272,128]{2,1,0:T(8,128)S(1)} all-to-all(f32[8,272,128]{2,1,0:T(8,128)S(1)} %shard_map.50.sent_ref), channel_id=1, replica_groups=mesh['far'=8,'near'=2,'x'=4,'y'=4,'core'=2] {'near','x'}, dimensions={0} | all-to-all | bytes 2228224 | tf_op jit(solution)/shard_map/all_to_all | solution.py:136
  25.7 0.2 reshape.42
  25.9 0.2 copy.23
  26.1 0.2 reshape.43
  26.4 31.2 %all_to_all.26 = f32[8,48,128]{2,1,0:T(8,128)S(1)} all-to-all(f32[8,48,128]{2,1,0:T(8,128)S(1)} %pad_maximum_fusion), channel_id=1, replica_groups=mesh['far'=8,'near'=2,'x'=4,'y'=4,'core'=2] {'far'}, dimensions={0} | all-to-all | bytes 393216 | tf_op jit(solution)/shard_map/all_to_all | solution.py:139
  57.7 0.1 reshape.44
  57.8 0.2 fusion
  58.1 0.1 convolution_bitcast_fusion
  58.4 13.6 %all_to_all.27 = f32[8,24,128]{2,1,0:T(8,128)S(1)} all-to-all(f32[8,24,128]{2,1,0:T(8,128)S(1)} %broadcast_in_dim.10), channel_id=1, replica_groups=mesh['far'=8,'near'=2,'x'=4,'y'=4,'core'=2] {'y','core'}, dimensions={0} | all-to-all | bytes 196608 | tf_op jit(solution)/shard_map/all_to_all | solution.py:19
  72.3 2.9 %cholesky.16 = f32[32,32]{1,0:T(8,128)S(1)} custom-call(f32[32,32]{1,0:T(8,128)S(1)} %fusion.8), custom_call_target="Cholesky" | custom-call | tf_op jit(solution)/shard_map/jit(cholesky)/cholesky | solution.py:150
  75.2 0.6 compare_reduce_fusion
  75.9 0.7 fusion.4
  76.5 2.4 %custom-call.8 = f32[1,32,32]{1,2,0:T(8,128)S(1)} custom-call(f32[1,32,32]{2,1,0:T(8,128)S(1)} %fusion.4), custom_call_target="InvertDiagBlocksLowerTriangular" | custom-call | tf_op jit(solution)/shard_map/triangular_solve | solution.py:151
  79.0 0.7 broadcast_in_dim.11
  79.6 3.4 %all-to-all-start.3 = ((f32[8,16,128]{2,1,0:T(8,128)}), f32[8,16,128]{2,1,0:T(8,128)S(1)}, u32[]{:S(2)}, u32[]{:S(2)}) async-start(f32[8,16,128]{2,1,0:T(8,128)} %broadcast_in_dim.11), calls=%async_computation.3 | async-start | bytes 131072 | tf_op jit(solution)/shard_map/all_to_all | solution.py:19
  83.0 0.2 fusion.6
  83.2 0.2 convolution_multiply_fusion.back_ref
  83.5 11.7 %all-to-all-done.3 = f32[8,16,128]{2,1,0:T(8,128)S(1)} async-done(((f32[8,16,128]{2,1,0:T(8,128)}), f32[8,16,128]{2,1,0:T(8,128)S(1)}, u32[]{:S(2)}, u32[]{:S(2)}) %all-to-all-start.3) | async-done | bytes 65568 | tf_op jit(solution)/shard_map/all_to_all | solution.py:19
  95.2 9.9 %all_to_all.28.whole_ref = f32[8,8,16,128]{3,2,1,0:T(8,128)S(1)} all-to-all(f32[8,8,16,128]{3,2,1,0:T(8,128)S(1)} %broadcast_in_dim.12), channel_id=1, replica_groups=mesh['far'=8,'near'=2,'x'=4,'y'=4,'core'=2] {'near','x'}, dimensions={0} | all-to-all | bytes 1048576 | tf_op jit(solution)/shard_map/all_to_all | solution.py:19
  105.1 2.9 %shard_map.51 = (f32[64,4096]{1,0:T(8,128)}, f32[1,64,4096]{2,1,0:T(8,128)}) custom-call(f32[64,32]{1,0:T(8,128)S(1)} %convolution_multiply_fusion.back_ref, f32[8,8,16,128]{3,2,1,0:T(8,128)S(1)} %all_to_all.28.whole_ref, f32[8,272,128]{2,1,0:T(8,128)S(1)} %shard_map.50.sent_ref), custom_call_target="tpu_custom_call" | custom-call | tf_op jit(solution)/shard_map/pallas_call | solution.py:109
  (27 shorter events, 0.7 us)
Async XLA Ops:
  0.6 1.2 %copy-start = (f32[1,64,4096]{2,1,0:T(8,128)S(1)}, f32[1,64,4096]{2,1,0:T(8,128)}, u32[]{:S(2)}) copy-start(f32[1,64,4096]{2,1,0:T(8,128)} %gradient_ref.1) | copy-start | bytes 3145732
  1.9 1.2 %copy-start.1 = (f32[1,64,4096]{2,1,0:T(8,128)S(1)}, f32[1,64,4096]{2,1,0:T(8,128)}, u32[]{:S(2)}) copy-start(f32[1,64,4096]{2,1,0:T(8,128)} %error_ref.1) | copy-start | bytes 3145732
  3.1 1.0 copy-start.2
  79.6 15.5 %all-to-all-start.3 = ((f32[8,16,128]{2,1,0:T(8,128)}), f32[8,16,128]{2,1,0:T(8,128)S(1)}, u32[]{:S(2)}, u32[]{:S(2)}) async-start(f32[8,16,128]{2,1,0:T(8,128)} %broadcast_in_dim.11), calls=%async_computation.3 | async-start | bytes 131072 | tf_op jit(solution)/shard_map/all_to_all | solution.py:19

commit v4 on v2

v4 whole, which is shorter than its diff:
```python
import functools

import jax
import jax.numpy as jnp
from jax import lax
from jax.experimental import pallas as pl
from jax.experimental.pallas import tpu as pltpu
from jax.sharding import Mesh, PartitionSpec as P

AXES = ("far", "near", "x", "y", "core")
DP = ("far", "near", "x")
TENSOR = ("y", "core")
CLOSE = ("near", "x")
HIGHEST = lax.Precision.HIGHEST
LANES = 128
SOME_VMEM = 16 * 2**20


def copies(block, axis):
    count = lax.axis_size(axis)
    return lax.all_to_all(jnp.broadcast_to(block[None], (count,) + block.shape), axis, 0, 0)


def pack(matrix):
    rows = matrix.shape[0]
    return matrix.reshape(4, rows // 4, 32).transpose(1, 0, 2).reshape(rows // 4, 128)


def unpack(dense):
    rows = dense.shape[0]
    return dense.reshape(rows, 4, 32).transpose(1, 0, 2).reshape(rows * 4, 32)


def beside(blocks, small):
    return jnp.concatenate([blocks, jnp.broadcast_to(small[None], blocks.shape[:1] + small.shape)], axis=1)


def first_kernel(corrected_ref, right_ref, sent_ref):
    rows, width = corrected_ref.shape
    rank, count = right_ref.shape[0], sent_ref.shape[0]
    span = width // count
    tiles = span // LANES
    total = None
    for block in range(count):
        columns = slice(block * span, (block + 1) * span)
        corrected = corrected_ref[:, columns]
        for tile in range(tiles):
            sent_ref[block, tile * rows : (tile + 1) * rows, :] = corrected[:, tile * LANES : (tile + 1) * LANES]
        part = lax.dot_general(
            corrected, right_ref[:, columns], (((1,), (1,)), ((), ())), precision=HIGHEST, preferred_element_type=jnp.float32
        )
        total = part if total is None else total + part
    groups = LANES // rank
    high = rows // groups
    dense = jnp.concatenate([total[g * high : (g + 1) * high, :] for g in range(groups)], axis=1)
    for block in range(count):
        sent_ref[block, tiles * rows :, :] = dense


def first(corrected, right, blocks):
    rank, width = right.shape
    rows = corrected.shape[0]
    height = rows * (width // blocks) // LANES + rows * rank // LANES
    near = pl.BlockSpec(memory_space=pltpu.VMEM)
    return pl.pallas_call(
        first_kernel,
        in_specs=[near, near],
        out_specs=near,
        out_shape=jax.ShapeDtypeStruct((blocks, height, LANES), jnp.float32),
        compiler_params=pltpu.CompilerParams(vmem_limit_bytes=SOME_VMEM),
    )(corrected, right)


def solve_kernel(gram_ref, left_ref, back_ref, *, replicas):
    rank = left_ref.shape[1]
    small = gram_ref[0]
    for peer in range(1, gram_ref.shape[0]):
        small += gram_ref[peer]
    gram = jnp.concatenate([small[:, g * rank : (g + 1) * rank] for g in range(LANES // rank)], axis=0)
    row_of = lax.broadcasted_iota(jnp.int32, (rank, rank), 0)
    unit = row_of == lax.broadcasted_iota(jnp.int32, (rank, rank), 1)
    both = jnp.concatenate([gram, unit.astype(jnp.float32)], axis=1)
    below = lax.broadcasted_iota(jnp.int32, (rank, 1), 0)
    for k in range(rank):
        factor = jnp.where(below > k, both[:, k : k + 1], 0.0) / both[k : k + 1, k : k + 1]
        both = both - factor * both[k : k + 1, :]
    pivots = jnp.sum(jnp.where(unit, both[:, :rank], 0.0), axis=0, keepdims=True)
    inverse = both[:, rank:]
    basis = lax.dot_general(
        left_ref[...], inverse, (((1,), (1,)), ((), ())), precision=HIGHEST, preferred_element_type=jnp.float32
    )
    basis = basis / (pivots * replicas)
    back_ref[...] = jnp.dot(basis, inverse, precision=HIGHEST, preferred_element_type=jnp.float32)


def solve(gram, left_sum, replicas):
    peers, height, lanes = gram.shape
    rows, rank = left_sum.shape
    high = rank * rank // LANES
    return pl.pallas_call(
        functools.partial(solve_kernel, replicas=float(replicas)),
        grid=(1,),
        in_specs=[
            pl.BlockSpec((peers, high, lanes), lambda i: (0, height // high - 1, 0)),
            pl.BlockSpec((rows, rank), lambda i: (0, 0)),
        ],
        out_specs=pl.BlockSpec((rows, rank), lambda i: (0, 0)),
        out_shape=jax.ShapeDtypeStruct((rows, rank), jnp.float32),
        compiler_params=pltpu.CompilerParams(vmem_limit_bytes=SOME_VMEM),
        cost_estimate=pl.CostEstimate(flops=4 * rank**3, bytes_accessed=2 * rows * LANES * 4, transcendentals=rank * rank),
    )(gram, left_sum)


def last_kernel(back_ref, whole_ref, sent_ref, averaged_ref, error_ref, averaged, error, leave):
    rows = back_ref.shape[0]
    count, pairs = whole_ref.shape[0], whole_ref.shape[1] // 2
    span = pairs * LANES
    low = lax.broadcasted_iota(jnp.int32, whole_ref.shape[2:], 1) < LANES // 2
    going = []
    for block in range(count):
        upper, lower = [], []
        for pair in range(pairs):
            even, odd = whole_ref[block, 2 * pair], whole_ref[block, 2 * pair + 1]
            upper.append(jnp.where(low, even, pltpu.roll(odd, LANES // 2, 1)))
            lower.append(jnp.where(low, pltpu.roll(even, LANES // 2, 1), odd))
        right = jnp.concatenate([jnp.concatenate(upper, axis=1), jnp.concatenate(lower, axis=1)], axis=0)
        columns = pl.ds(block * span, span)
        found = jnp.dot(back_ref[...], right, precision=HIGHEST, preferred_element_type=jnp.float32)
        averaged[block] = found
        for tile in range(pairs):
            lanes = slice(tile * LANES, (tile + 1) * LANES)
            error[block, :, lanes] = sent_ref[block, tile * rows : (tile + 1) * rows, :] - found[:, lanes]
        going.append(pltpu.make_async_copy(averaged.at[block], averaged_ref.at[:, columns], leave.at[0, block]))
        going.append(pltpu.make_async_copy(error.at[block], error_ref.at[0, :, columns], leave.at[1, block]))
        going[-2].start()
        going[-1].start()
    for copy in going:
        copy.wait()


def last(back, whole, sent):
    rows = back.shape[0]
    blocks = sent.shape[0]
    span = whole.shape[1] * LANES // 2
    near, anywhere = pl.BlockSpec(memory_space=pltpu.VMEM), pl.BlockSpec(memory_space=pl.ANY)
    return pl.pallas_call(
        last_kernel,
        in_specs=[near, near, near],
        out_specs=[anywhere, anywhere],
        out_shape=[
            jax.ShapeDtypeStruct((rows, blocks * span), jnp.float32),
            jax.ShapeDtypeStruct((1, rows, blocks * span), jnp.float32),
        ],
        scratch_shapes=[
            pltpu.VMEM((blocks, rows, span), jnp.float32),
            pltpu.VMEM((blocks, rows, span), jnp.float32),
            pltpu.SemaphoreType.DMA((2, blocks)),
        ],
        compiler_params=pltpu.CompilerParams(vmem_limit_bytes=SOME_VMEM),
    )(back, whole, sent)


def shards(gradient, error_buffer, right_factor):
    width, rank = right_factor.shape
    rows = gradient.shape[1]
    close, far = lax.axis_size(CLOSE), lax.axis_size("far")
    tiles = width // close // LANES

    corrected = gradient[0] + error_buffer[0]
    sent = first(corrected, right_factor.T, close)
    got = lax.all_to_all(sent, CLOSE, 0, 0).sum(0)
    blocks = got[: tiles * rows].reshape(tiles, 2, rows // 2, 2, LANES // 2).transpose(0, 3, 2, 1, 4)
    blocks = blocks.reshape(far, rows // 2, LANES)
    got = lax.all_to_all(beside(blocks, got[tiles * rows :]), "far", 0, 0).sum(0)
    left_sum = unpack(got[rows // 2 :])
    own = jnp.concatenate([got[: rows // 2, : LANES // 2], got[: rows // 2, LANES // 2 :]], axis=0)

    part = lax.dot_general(left_sum, own, (((0,), (0,)), ((), ())), precision=HIGHEST)
    part = jnp.concatenate([part[: rank // 2], part[rank // 2 :]], axis=1)
    gram = pack(lax.dot_general(left_sum, left_sum, (((0,), (0,)), ((), ())), precision=HIGHEST))
    got = copies(jnp.concatenate([part, gram], axis=0), TENSOR)
    back = solve(got, left_sum, lax.axis_size(DP))
    whole = copies(copies(got[:, : rank // 2].sum(0), "far"), CLOSE)
    averaged, new_error = last(back, whole, sent)
    return (averaged, new_error)


def solution(mesh):
    fine = Mesh(mesh.devices.reshape(8, 2, 4, 4, 2), AXES)
    in_specs = (P(DP, TENSOR, None), P(DP, TENSOR, None), P())
    out_specs = (P(TENSOR, None), P(DP, TENSOR, None))
    return jax.shard_map(shards, mesh=fine, in_specs=in_specs, out_specs=out_specs, check_vma=False)
```

time: 106 us -> 98.1 us (0.925); the launches traced: 106 us -> 96.7 us
  blocking collectives: 30.9 us -> 78.4 us
  starting transfers between devices: 38.9 us -> 3.49 us
  waiting for transfers between devices: 19.2 us -> 4.03 us
  other arithmetic: 9.66 us -> 1.89 us
  Pallas kernels: 0 us -> 5.95 us
  matrix products: 2.8 us -> 0.36 us
  local copies, waits for them, and re-layouts: 3.57 us -> 1.78 us
    all_to_all x1 -> x2, blocking collectives: 16.2 us -> 50.3 us  [the longest x1 31.2 us: shards(): got = lax.all_to_all(beside(blocks, got[tiles * rows:]), 'far', 0, 0).sum(0)]
    all_to_all x3 -> x1, starting transfers between devices: 30.4 us -> 3.49 us  [copies(): lax.all_to_all(jnp.broadcast_to(block[None], (count,) + block.shape), axi...]
    all_to_all x1 -> x2, blocking collectives: 8.93 us -> 28.1 us  [copies(): lax.all_to_all(jnp.broadcast_to(block[None], (count,) + block.shape), axi...]
    all_to_all x3 -> x1, waiting for transfers between devices: 16.2 us -> 4.03 us  [copies(): lax.all_to_all(jnp.broadcast_to(block[None], (count,) + block.shape), axi...]
    ppermute x3 -> x0, starting transfers between devices: 8.41 us -> none  [shards(): moved = moved + lax.ppermute(block(step), 'x', ring)]
    another operation x5 -> x0, other arithmetic: 6.67 us -> none  [the longest x3 3.59 us: shards(): lower = jnp.linalg.cholesky(gram)]
    pallas_call x0 -> x3, Pallas kernels: none -> 5.95 us  [the longest x1 3.03 us: solve(): pl.pallas_call(functools.partial(solve_kernel, replicas=float(replicas)),...]
    all_gather x1 -> x0, blocking collectives: 5.75 us -> none  [shards(): whole = lax.all_gather(copies(mine, ('near', 'x', 'y')), 'core')]
  transfers between devices with their start and end apart: 6 -> 1, of which waited for: 4 -> 1; matrix products, arithmetic and copies ran while one was open for 7% -> 0% of each run, Pallas kernels for 0% -> 3%
where the time goes in v4:
time: 98.1 us; the launch traced here: 96.7 us
  blocking collectives  78.4 us (80%)
  Pallas kernels  5.95 us (6%)
  waiting for transfers between devices  4.03 us (4%)
  starting transfers between devices  3.49 us (4%)
  other arithmetic  1.89 us (2%)
  local copies, waits for them, and re-layouts  1.78 us (2%)
    all_to_all x1, blocking collectives, shards(): got = lax.all_to_all(beside(blocks, got[tiles * rows:]), 'far', 0, 0).sum(0)  31.2 us
    all_to_all x2, blocking collectives, copies(): lax.all_to_all(jnp.broadcast_to(block[None], (count,) + block.shape), axi...  28.1 us
    all_to_all x1, blocking collectives, shards(): got = lax.all_to_all(sent, CLOSE, 0, 0).sum(0)  19.1 us
    all_to_all x1, waiting for transfers between devices, copies(): lax.all_to_all(jnp.broadcast_to(block[None], (count,) + block.shape), axi...  4.03 us
    all_to_all x1, starting transfers between devices, copies(): lax.all_to_all(jnp.broadcast_to(block[None], (count,) + block.shape), axi...  3.49 us
    pallas_call x1, Pallas kernels, solve(): pl.pallas_call(functools.partial(solve_kernel, replicas=float(replicas)),...  3.03 us
  transfers between devices with their start and end apart: 1, of which 1 were waited for; matrix products, arithmetic and copies ran while one was open for 0% of the time, Pallas kernels for 3%

profile of v4, /device:TPU:1, one launch (start us, length us, event | category | flops | bytes accessed | tf_op | source)
XLA Modules:
  0.0 96.7 jit_solution(14701432066983838778)
XLA Ops:
  0.6 0.0 copy-start
  0.6 1.7 %add_bitcast_fusion.corrected_ref = f32[64,4096]{1,0:T(8,128)S(1)} fusion(f32[1,64,4096]{2,1,0:T(8,128)} %param.3, f32[1,64,4096]{2,1,0:T(8,128)} %param.4), kind=kLoop, calls=%fused_computation.1 | loop fusion | flops 262144 | bytes 3145728 | tf_op jit(solution)/shard_map/add | solution.py:169
  2.3 0.0 copy-done
  2.4 1.0 %shard_map.50.sent_ref = f32[8,272,128]{2,1,0:T(8,128)S(1)} custom-call(f32[64,4096]{1,0:T(8,128)S(1)} %add_bitcast_fusion.corrected_ref, f32[32,4096]{1,0:T(8,128)S(1)} %bitcast.21), custom_call_target="tpu_custom_call" | custom-call | tf_op jit(solution)/shard_map/pallas_call | solution.py:65
  3.4 19.1 %all_to_all.25 = f32[8,272,128]{2,1,0:T(8,128)S(1)} all-to-all(f32[8,272,128]{2,1,0:T(8,128)S(1)} %shard_map.50.sent_ref), channel_id=1, replica_groups=mesh['far'=8,'near'=2,'x'=4,'y'=4,'core'=2] {'near','x'}, dimensions={0} | all-to-all | bytes 2228224 | tf_op jit(solution)/shard_map/all_to_all | solution.py:171
  22.5 0.1 reduce_sum.27
  22.6 0.2 reshape.26
  22.8 0.2 copy.10
  23.0 0.2 reshape.27
  23.2 31.2 %all_to_all.26 = f32[8,48,128]{2,1,0:T(8,128)S(1)} all-to-all(f32[8,48,128]{2,1,0:T(8,128)S(1)} %pad_maximum_fusion), channel_id=1, replica_groups=mesh['far'=8,'near'=2,'x'=4,'y'=4,'core'=2] {'far'}, dimensions={0} | all-to-all | bytes 393216 | tf_op jit(solution)/shard_map/all_to_all | solution.py:174
  54.4 0.1 fusion.6
  54.5 0.1 reshape.28
  54.6 0.2 fusion
  54.9 0.1 copy.12
  54.9 0.1 convolution_bitcast_fusion
  55.1 0.1 reshape.30
  55.2 0.1 pad_maximum_fusion.1
  55.3 13.6 %all_to_all.27.gram_ref = f32[8,24,128]{2,1,0:T(8,128)S(1)} all-to-all(f32[8,24,128]{2,1,0:T(8,128)S(1)} %broadcast_in_dim.9), channel_id=1, replica_groups=mesh['far'=8,'near'=2,'x'=4,'y'=4,'core'=2] {'y','core'}, dimensions={0} | all-to-all | bytes 196608 | tf_op jit(solution)/shard_map/all_to_all | solution.py:21
  68.9 14.5 %all_to_all.28 = f32[8,16,128]{2,1,0:T(8,128)S(1)} all-to-all(f32[8,16,128]{2,1,0:T(8,128)S(1)} %broadcast_in_dim.10), channel_id=1, replica_groups=mesh['far'=8,'near'=2,'x'=4,'y'=4,'core'=2] {'far'}, dimensions={0} | all-to-all | bytes 131072 | tf_op jit(solution)/shard_map/all_to_all | solution.py:21
  83.4 0.8 broadcast_in_dim.11
  84.3 3.5 %all-to-all-start.4 = ((f32[8,8,16,128]{3,2,1,0:T(8,128)}), f32[8,8,16,128]{3,2,1,0:T(8,128)S(1)}, u32[]{:S(2)}, u32[]{:S(2)}) async-start(f32[8,8,16,128]{3,2,1,0:T(8,128)} %broadcast_in_dim.11), calls=%async_computation.4 | async-start | bytes 1048576 | tf_op jit(solution)/shard_map/all_to_all | solution.py:21
  87.8 3.0 %shard_map.51.back_ref = f32[64,32]{1,0:T(8,128)S(1)} custom-call(f32[8,24,128]{2,1,0:T(8,128)S(1)} %all_to_all.27.gram_ref, f32[64,32]{1,0:T(8,128)S(1)} %bitcast.20), custom_call_target="tpu_custom_call" | custom-call | flops 131072 | bytes 65536 | tf_op jit(solution)/shard_map/pallas_call | solution.py:100
  90.8 4.0 %all-to-all-done.4.whole_ref = f32[8,8,16,128]{3,2,1,0:T(8,128)S(1)} async-done(((f32[8,8,16,128]{3,2,1,0:T(8,128)}), f32[8,8,16,128]{3,2,1,0:T(8,128)S(1)}, u32[]{:S(2)}, u32[]{:S(2)}) %all-to-all-start.4) | async-done | bytes 524320 | tf_op jit(solution)/shard_map/all_to_all | solution.py:21
  94.8 1.9 %shard_map.52 = (f32[64,4096]{1,0:T(8,128)}, f32[1,64,4096]{2,1,0:T(8,128)}) custom-call(f32[64,32]{1,0:T(8,128)S(1)} %shard_map.51.back_ref, f32[8,8,16,128]{3,2,1,0:T(8,128)S(1)} %all-to-all-done.4.whole_ref, f32[8,272,128]{2,1,0:T(8,128)S(1)} %shard_map.50.sent_ref), custom_call_target="tpu_custom_call" | custom-call | tf_op jit(solution)/shard_map/pallas_call | solution.py:146
  (12 shorter events, 0.1 us)
Async XLA Ops:
  0.6 1.7 %copy-start = (f32[4096,32]{0,1:T(8,128)S(1)}, f32[4096,32]{0,1:T(8,128)}, u32[]{:S(2)}) copy-start(f32[4096,32]{0,1:T(8,128)} %param.5) | copy-start | bytes 1572868
  84.3 10.6 %all-to-all-start.4 = ((f32[8,8,16,128]{3,2,1,0:T(8,128)}), f32[8,8,16,128]{3,2,1,0:T(8,128)S(1)}, u32[]{:S(2)}, u32[]{:S(2)}) async-start(f32[8,8,16,128]{3,2,1,0:T(8,128)} %broadcast_in_dim.11), calls=%async_computation.4 | async-start | bytes 1048576 | tf_op jit(solution)/shard_map/all_to_all | solution.py:21

commit v5 on v4

--- a/solution.py
+++ b/solution.py
@@ -19,20 +19,6 @@
 def copies(block, axis):
     count = lax.axis_size(axis)
     return lax.all_to_all(jnp.broadcast_to(block[None], (count,) + block.shape), axis, 0, 0)
-
-
-def pack(matrix):
-    rows = matrix.shape[0]
-    return matrix.reshape(4, rows // 4, 32).transpose(1, 0, 2).reshape(rows // 4, 128)
-
-
-def unpack(dense):
-    rows = dense.shape[0]
-    return dense.reshape(rows, 4, 32).transpose(1, 0, 2).reshape(rows * 4, 32)
-
-
-def beside(blocks, small):
-    return jnp.concatenate([blocks, jnp.broadcast_to(small[None], blocks.shape[:1] + small.shape)], axis=1)
 
 
 def first_kernel(corrected_ref, right_ref, sent_ref):
@@ -69,6 +55,78 @@
         out_shape=jax.ShapeDtypeStruct((blocks, height, LANES), jnp.float32),
         compiler_params=pltpu.CompilerParams(vmem_limit_bytes=SOME_VMEM),
     )(corrected, right)
+
+
+def halve_kernel(got_ref, sent_ref):
+    count, high = sent_ref.shape[0], got_ref.shape[1]
+    half = LANES // 2
+    tiles = count // 2
+    small = sent_ref.shape[1] // 3
+    rows = (high - small) // tiles
+
+    def total(start, size):
+        found = got_ref[0, start : start + size, :]
+        for peer in range(1, got_ref.shape[0]):
+            found += got_ref[peer, start : start + size, :]
+        return found
+
+    left = total(tiles * rows, small)
+    low = lax.broadcasted_iota(jnp.int32, (rows // 2, LANES), 1) < half
+    for tile in range(tiles):
+        upper, lower = total(tile * rows, rows // 2), total(tile * rows + rows // 2, rows // 2)
+        sent_ref[2 * tile, : rows // 2, :] = jnp.where(low, upper, pltpu.roll(lower, half, 1))
+        sent_ref[2 * tile + 1, : rows // 2, :] = jnp.where(low, pltpu.roll(upper, half, 1), lower)
+        sent_ref[2 * tile, rows // 2 :, :] = left
+        sent_ref[2 * tile + 1, rows // 2 :, :] = left
+
+
+def halve(got, rows, small, pairs):
+    near = pl.BlockSpec(memory_space=pltpu.VMEM)
+    return pl.pallas_call(
+        halve_kernel,
+        in_specs=[near],
+        out_specs=near,
+        out_shape=jax.ShapeDtypeStruct((pairs, rows // 2 + small, LANES), jnp.float32),
+        compiler_params=pltpu.CompilerParams(vmem_limit_bytes=SOME_VMEM),
+    )(got)
+
+
+def middle_kernel(got_ref, sent_ref, left_ref):
+    rows, rank = left_ref.shape
+    half, groups = LANES // 2, LANES // rank
+    found = got_ref[0]
+    for peer in range(1, got_ref.shape[0]):
+        found += got_ref[peer]
+    own, dense = found[: rows // 2, :], found[rows // 2 :, :]
+    left = jnp.concatenate([dense[:, g * rank : (g + 1) * rank] for g in range(groups)], axis=0)
+    left_ref[...] = left
+    turned = left.T
+    upper = jnp.dot(turned[:, : rows // 2], own, precision=HIGHEST, preferred_element_type=jnp.float32)
+    lower = jnp.dot(turned[:, rows // 2 :], own, precision=HIGHEST, preferred_element_type=jnp.float32)
+    first = upper + pltpu.roll(lower, half, 1)
+    second = pltpu.roll(upper, half, 1) + lower
+    low = lax.broadcasted_iota(jnp.int32, (rank // 2, LANES), 1) < half
+    part = jnp.where(low, first[: rank // 2, :], second[rank // 2 :, :])
+    gram = jnp.dot(turned, left, precision=HIGHEST, preferred_element_type=jnp.float32)
+    high = rank // groups
+    gram = jnp.concatenate([gram[g * high : (g + 1) * high, :] for g in range(groups)], axis=1)
+    for peer in range(sent_ref.shape[0]):
+        sent_ref[peer, : rank // 2, :] = part
+        sent_ref[peer, rank // 2 :, :] = gram
+
+
+def middle(got, rows, rank, peers):
+    near = pl.BlockSpec(memory_space=pltpu.VMEM)
+    return pl.pallas_call(
+        middle_kernel,
+        in_specs=[near],
+        out_specs=[near, near],
+        out_shape=[
+            jax.ShapeDtypeStruct((peers, rank // 2 + rank * rank // LANES, LANES), jnp.float32),
+            jax.ShapeDtypeStruct((rows, rank), jnp.float32),
+        ],
+        compiler_params=pltpu.CompilerParams(vmem_limit_bytes=SOME_VMEM),
+    )(got)
 
 
 def solve_kernel(gram_ref, left_ref, back_ref, *, replicas):
@@ -161,24 +219,17 @@
 
 
 def shards(gradient, error_buffer, right_factor):
-    width, rank = right_factor.shape
+    rank = right_factor.shape[1]
     rows = gradient.shape[1]
     close, far = lax.axis_size(CLOSE), lax.axis_size("far")
-    tiles = width // close // LANES
 
     corrected = gradient[0] + error_buffer[0]
     sent = first(corrected, right_factor.T, close)
-    got = lax.all_to_all(sent, CLOSE, 0, 0).sum(0)
-    blocks = got[: tiles * rows].reshape(tiles, 2, rows // 2, 2, LANES // 2).transpose(0, 3, 2, 1, 4)
-    blocks = blocks.reshape(far, rows // 2, LANES)
-    got = lax.all_to_all(beside(blocks, got[tiles * rows :]), "far", 0, 0).sum(0)
-    left_sum = unpack(got[rows // 2 :])
-    own = jnp.concatenate([got[: rows // 2, : LANES // 2], got[: rows // 2, LANES // 2 :]], axis=0)
-
-    part = lax.dot_general(left_sum, own, (((0,), (0,)), ((), ())), precision=HIGHEST)
-    part = jnp.concatenate([part[: rank // 2], part[rank // 2 :]], axis=1)
-    gram = pack(lax.dot_general(left_sum, left_sum, (((0,), (0,)), ((), ())), precision=HIGHEST))
-    got = copies(jnp.concatenate([part, gram], axis=0), TENSOR)
+    got = lax.all_to_all(sent, CLOSE, 0, 0)
+    got = lax.all_to_all(halve(got, rows, rows * rank // LANES, far), "far", 0, 0)
+
+    got, left_sum = middle(got, rows, rank, lax.axis_size(TENSOR))
+    got = lax.all_to_all(got, TENSOR, 0, 0)
     back = solve(got, left_sum, lax.axis_size(DP))
     whole = copies(copies(got[:, : rank // 2].sum(0), "far"), CLOSE)
     averaged, new_error = last(back, whole, sent)

time: 98.1 us -> 97.1 us (0.990)
    all_to_all x2 -> x3, blocking collectives: 50.3 us -> 64 us  [the longest x1 31.2 us: shards(): lax.all_to_all(halve(got, rows, rows * rank // LANES, far), 'far', 0, 0)]
    all_to_all x2 -> x1, blocking collectives: 28.1 us -> 14.5 us  [copies(): lax.all_to_all(jnp.broadcast_to(block[None], (count,) + block.shape), axi...]
where the time goes in v5:
time: 97.1 us; the launch traced here: 95.7 us
  blocking collectives  78.4 us (81%)
  Pallas kernels  6.53 us (7%)
  waiting for transfers between devices  4.03 us (4%)
  starting transfers between devices  3.49 us (4%)
  other arithmetic  1.72 us (2%)
    all_to_all x1, blocking collectives, shards(): lax.all_to_all(halve(got, rows, rows * rank // LANES, far), 'far', 0, 0)  31.2 us
    all_to_all x1, blocking collectives, shards(): got = lax.all_to_all(sent, CLOSE, 0, 0)  19.1 us
    all_to_all x1, blocking collectives, copies(): lax.all_to_all(jnp.broadcast_to(block[None], (count,) + block.shape), axi...  14.5 us
    all_to_all x1, blocking collectives, shards(): got = lax.all_to_all(got, TENSOR, 0, 0)  13.7 us
    all_to_all x1, waiting for transfers between devices, copies(): lax.all_to_all(jnp.broadcast_to(block[None], (count,) + block.shape), axi...  4.03 us
    all_to_all x1, starting transfers between devices, copies(): lax.all_to_all(jnp.broadcast_to(block[None], (count,) + block.shape), axi...  3.49 us
    pallas_call x1, Pallas kernels, solve(): pl.pallas_call(functools.partial(solve_kernel, replicas=float(replicas)),...  3.03 us
  transfers between devices with their start and end apart: 1, of which 1 were waited for; matrix products, arithmetic and copies ran while one was open for 0% of the time, Pallas kernels for 3%

profile of v5, /device:TPU:1, one launch (start us, length us, event | category | flops | bytes accessed | tf_op | source)
XLA Modules:
  0.0 95.7 jit_solution(6674737136039797864)
XLA Ops:
  0.6 0.0 copy-start
  0.6 1.7 %add_bitcast_fusion.corrected_ref = f32[64,4096]{1,0:T(8,128)S(1)} fusion(f32[1,64,4096]{2,1,0:T(8,128)} %param.3, f32[1,64,4096]{2,1,0:T(8,128)} %param.4), kind=kLoop, calls=%fused_computation | loop fusion | flops 262144 | bytes 3145728 | tf_op jit(solution)/shard_map/add | solution.py:226
  2.3 0.0 copy-done
  2.4 1.0 %shard_map.50.sent_ref = f32[8,272,128]{2,1,0:T(8,128)S(1)} custom-call(f32[64,4096]{1,0:T(8,128)S(1)} %add_bitcast_fusion.corrected_ref, f32[32,4096]{1,0:T(8,128)S(1)} %bitcast.3), custom_call_target="tpu_custom_call" | custom-call | tf_op jit(solution)/shard_map/pallas_call | solution.py:51
  3.4 19.1 %all_to_all.25.got_ref = f32[8,272,128]{2,1,0:T(8,128)S(1)} all-to-all(f32[8,272,128]{2,1,0:T(8,128)S(1)} %shard_map.50.sent_ref), channel_id=1, replica_groups=mesh['far'=8,'near'=2,'x'=4,'y'=4,'core'=2] {'near','x'}, dimensions={0} | all-to-all | bytes 2228224 | tf_op jit(solution)/shard_map/all_to_all | solution.py:228
  22.5 0.1 shard_map.51
  22.6 31.2 %all_to_all.26.got_ref = f32[8,48,128]{2,1,0:T(8,128)S(1)} all-to-all(f32[8,48,128]{2,1,0:T(8,128)S(1)} %shard_map.51), channel_id=1, replica_groups=mesh['far'=8,'near'=2,'x'=4,'y'=4,'core'=2] {'far'}, dimensions={0} | all-to-all | bytes 393216 | tf_op jit(solution)/shard_map/all_to_all | solution.py:229
  53.8 0.5 shard_map.52
  54.3 13.7 %all_to_all.27.gram_ref = f32[8,24,128]{2,1,0:T(8,128)S(1)} all-to-all(f32[8,24,128]{2,1,0:T(8,128)S(1)} %get-tuple-element.4), channel_id=1, replica_groups=mesh['far'=8,'near'=2,'x'=4,'y'=4,'core'=2] {'y','core'}, dimensions={0} | all-to-all | bytes 196608 | tf_op jit(solution)/shard_map/all_to_all | solution.py:232
  68.0 14.5 %all_to_all.28 = f32[8,16,128]{2,1,0:T(8,128)S(1)} all-to-all(f32[8,16,128]{2,1,0:T(8,128)S(1)} %broadcast_in_dim.4), channel_id=1, replica_groups=mesh['far'=8,'near'=2,'x'=4,'y'=4,'core'=2] {'far'}, dimensions={0} | all-to-all | bytes 131072 | tf_op jit(solution)/shard_map/all_to_all | solution.py:21
  82.5 0.8 broadcast_in_dim.5
  83.3 3.5 %all-to-all-start.4 = ((f32[8,8,16,128]{3,2,1,0:T(8,128)}), f32[8,8,16,128]{3,2,1,0:T(8,128)S(1)}, u32[]{:S(2)}, u32[]{:S(2)}) async-start(f32[8,8,16,128]{3,2,1,0:T(8,128)} %broadcast_in_dim.5), calls=%async_computation.4 | async-start | bytes 1048576 | tf_op jit(solution)/shard_map/all_to_all | solution.py:21
  86.8 3.0 %shard_map.53.back_ref = f32[64,32]{1,0:T(8,128)S(1)} custom-call(f32[8,24,128]{2,1,0:T(8,128)S(1)} %all_to_all.27.gram_ref, f32[64,32]{1,0:T(8,128)S(1)} %get-tuple-element.5.left_ref), custom_call_target="tpu_custom_call" | custom-call | flops 131072 | bytes 65536 | tf_op jit(solution)/shard_map/pallas_call | solution.py:158
  89.8 4.0 %all-to-all-done.4.whole_ref = f32[8,8,16,128]{3,2,1,0:T(8,128)S(1)} async-done(((f32[8,8,16,128]{3,2,1,0:T(8,128)}), f32[8,8,16,128]{3,2,1,0:T(8,128)S(1)}, u32[]{:S(2)}, u32[]{:S(2)}) %all-to-all-start.4) | async-done | bytes 524320 | tf_op jit(solution)/shard_map/all_to_all | solution.py:21
  93.9 1.9 %shard_map.54 = (f32[64,4096]{1,0:T(8,128)}, f32[1,64,4096]{2,1,0:T(8,128)}) custom-call(f32[64,32]{1,0:T(8,128)S(1)} %shard_map.53.back_ref, f32[8,8,16,128]{3,2,1,0:T(8,128)S(1)} %all-to-all-done.4.whole_ref, f32[8,272,128]{2,1,0:T(8,128)S(1)} %shard_map.50.sent_ref), custom_call_target="tpu_custom_call" | custom-call | tf_op jit(solution)/shard_map/pallas_call | solution.py:204
  (2 shorter events, 0.0 us)
Async XLA Ops:
  0.6 1.7 %copy-start = (f32[4096,32]{0,1:T(8,128)S(1)}, f32[4096,32]{0,1:T(8,128)}, u32[]{:S(2)}) copy-start(f32[4096,32]{0,1:T(8,128)} %param.5) | copy-start | bytes 1572868
  83.3 10.6 %all-to-all-start.4 = ((f32[8,8,16,128]{3,2,1,0:T(8,128)}), f32[8,8,16,128]{3,2,1,0:T(8,128)S(1)}, u32[]{:S(2)}, u32[]{:S(2)}) async-start(f32[8,8,16,128]{3,2,1,0:T(8,128)} %broadcast_in_dim.5), calls=%async_computation.4 | async-start | bytes 1048576 | tf_op jit(solution)/shard_map/all_to_all | solution.py:21

commit v6 on v5

--- a/solution.py
+++ b/solution.py
@@ -110,9 +110,11 @@
     gram = jnp.dot(turned, left, precision=HIGHEST, preferred_element_type=jnp.float32)
     high = rank // groups
     gram = jnp.concatenate([gram[g * high : (g + 1) * high, :] for g in range(groups)], axis=1)
+    share = rank // 4
     for peer in range(sent_ref.shape[0]):
-        sent_ref[peer, : rank // 2, :] = part
-        sent_ref[peer, rank // 2 :, :] = gram
+        core = peer % 2
+        sent_ref[peer, :share, :] = part[core * share : (core + 1) * share, :]
+        sent_ref[peer, share:, :] = gram
 
 
 def middle(got, rows, rank, peers):
@@ -122,7 +124,7 @@
         in_specs=[near],
         out_specs=[near, near],
         out_shape=[
-            jax.ShapeDtypeStruct((peers, rank // 2 + rank * rank // LANES, LANES), jnp.float32),
+            jax.ShapeDtypeStruct((peers, rank // 4 + rank * rank // LANES, LANES), jnp.float32),
             jax.ShapeDtypeStruct((rows, rank), jnp.float32),
         ],
         compiler_params=pltpu.CompilerParams(vmem_limit_bytes=SOME_VMEM),
@@ -171,14 +173,18 @@
 
 def last_kernel(back_ref, whole_ref, sent_ref, averaged_ref, error_ref, averaged, error, leave):
     rows = back_ref.shape[0]
-    count, pairs = whole_ref.shape[0], whole_ref.shape[1] // 2
+    count, pairs = whole_ref.shape[1], whole_ref.shape[2] // 2
     span = pairs * LANES
-    low = lax.broadcasted_iota(jnp.int32, whole_ref.shape[2:], 1) < LANES // 2
+    low = lax.broadcasted_iota(jnp.int32, (2 * whole_ref.shape[3], LANES), 1) < LANES // 2
+
+    def of_both(block, at):
+        return jnp.concatenate([whole_ref[0, block, at], whole_ref[1, block, at]], axis=0)
+
     going = []
     for block in range(count):
         upper, lower = [], []
         for pair in range(pairs):
-            even, odd = whole_ref[block, 2 * pair], whole_ref[block, 2 * pair + 1]
+            even, odd = of_both(block, 2 * pair), of_both(block, 2 * pair + 1)
             upper.append(jnp.where(low, even, pltpu.roll(odd, LANES // 2, 1)))
             lower.append(jnp.where(low, pltpu.roll(even, LANES // 2, 1), odd))
         right = jnp.concatenate([jnp.concatenate(upper, axis=1), jnp.concatenate(lower, axis=1)], axis=0)
@@ -199,7 +205,7 @@
 def last(back, whole, sent):
     rows = back.shape[0]
     blocks = sent.shape[0]
-    span = whole.shape[1] * LANES // 2
+    span = whole.shape[2] * LANES // 2
     near, anywhere = pl.BlockSpec(memory_space=pltpu.VMEM), pl.BlockSpec(memory_space=pl.ANY)
     return pl.pallas_call(
         last_kernel,
@@ -231,7 +237,7 @@
     got, left_sum = middle(got, rows, rank, lax.axis_size(TENSOR))
     got = lax.all_to_all(got, TENSOR, 0, 0)
     back = solve(got, left_sum, lax.axis_size(DP))
-    whole = copies(copies(got[:, : rank // 2].sum(0), "far"), CLOSE)
+    whole = lax.all_gather(copies(copies(got[:, : rank // 4].sum(0), "far"), CLOSE), "core")
     averaged, new_error = last(back, whole, sent)
     return (averaged, new_error)
 

time: 97.1 us -> 99.2 us (1.022); the launches traced: 95.7 us -> 98.9 us
  blocking collectives: 78.4 us -> 82.8 us
  waiting for transfers between devices: 4.03 us -> 2.97 us
    all_gather x0 -> x1, blocking collectives: none -> 4.88 us  [shards(): lax.all_gather(copies(copies(got[:, :rank // 4].sum(0), 'far'), CLOSE), '...]
    all_to_all x1, waiting for transfers between devices: 4.03 us -> 2.97 us  [copies(): lax.all_to_all(jnp.broadcast_to(block[None], (count,) + block.shape), axi...]
where the time goes in v6:
time: 99.2 us; the launch traced here: 98.9 us
  blocking collectives  82.8 us (83%)
  Pallas kernels  6.51 us (7%)
  starting transfers between devices  3.41 us (3%)
  waiting for transfers between devices  2.97 us (3%)
  other arithmetic  1.72 us (2%)
    all_to_all x1, blocking collectives, shards(): lax.all_to_all(halve(got, rows, rows * rank // LANES, far), 'far', 0, 0)  31.2 us
    all_to_all x1, blocking collectives, shards(): got = lax.all_to_all(sent, CLOSE, 0, 0)  19.1 us
    all_to_all x1, blocking collectives, copies(): lax.all_to_all(jnp.broadcast_to(block[None], (count,) + block.shape), axi...  14.1 us
    all_to_all x1, blocking collectives, shards(): got = lax.all_to_all(got, TENSOR, 0, 0)  13.5 us
    all_gather x1, blocking collectives, shards(): lax.all_gather(copies(copies(got[:, :rank // 4].sum(0), 'far'), CLOSE), '...  4.88 us
    all_to_all x1, starting transfers between devices, copies(): lax.all_to_all(jnp.broadcast_to(block[None], (count,) + block.shape), axi...  3.41 us
    pallas_call x1, Pallas kernels, solve(): pl.pallas_call(functools.partial(solve_kernel, replicas=float(replicas)),...  3.03 us
    all_to_all x1, waiting for transfers between devices, copies(): lax.all_to_all(jnp.broadcast_to(block[None], (count,) + block.shape), axi...  2.97 us
  transfers between devices with their start and end apart: 1, of which 1 were waited for; matrix products, arithmetic and copies ran while one was open for 0% of the time, Pallas kernels for 3%

profile of v6, /device:TPU:1, one launch (start us, length us, event | category | flops | bytes accessed | tf_op | source)
XLA Modules:
  0.0 98.9 jit_solution(9833798971768210792)
XLA Ops:
  0.6 0.0 copy-start
  0.6 1.7 %add_bitcast_fusion.corrected_ref = f32[64,4096]{1,0:T(8,128)S(1)} fusion(f32[1,64,4096]{2,1,0:T(8,128)} %param.3, f32[1,64,4096]{2,1,0:T(8,128)} %param.4), kind=kLoop, calls=%fused_computation | loop fusion | flops 262144 | bytes 3145728 | tf_op jit(solution)/shard_map/add | solution.py:232
  2.3 0.0 copy-done
  2.4 1.0 %shard_map.50.sent_ref = f32[8,272,128]{2,1,0:T(8,128)S(1)} custom-call(f32[64,4096]{1,0:T(8,128)S(1)} %add_bitcast_fusion.corrected_ref, f32[32,4096]{1,0:T(8,128)S(1)} %bitcast.5), custom_call_target="tpu_custom_call" | custom-call | tf_op jit(solution)/shard_map/pallas_call | solution.py:51
  3.4 19.1 %all_to_all.25.got_ref = f32[8,272,128]{2,1,0:T(8,128)S(1)} all-to-all(f32[8,272,128]{2,1,0:T(8,128)S(1)} %shard_map.50.sent_ref), channel_id=1, replica_groups=mesh['far'=8,'near'=2,'x'=4,'y'=4,'core'=2] {'near','x'}, dimensions={0} | all-to-all | bytes 2228224 | tf_op jit(solution)/shard_map/all_to_all | solution.py:234
  22.5 0.1 shard_map.51
  22.6 31.2 %all_to_all.26.got_ref = f32[8,48,128]{2,1,0:T(8,128)S(1)} all-to-all(f32[8,48,128]{2,1,0:T(8,128)S(1)} %shard_map.51), channel_id=1, replica_groups=mesh['far'=8,'near'=2,'x'=4,'y'=4,'core'=2] {'far'}, dimensions={0} | all-to-all | bytes 393216 | tf_op jit(solution)/shard_map/all_to_all | solution.py:235
  53.8 0.4 shard_map.52
  54.3 13.5 %all_to_all.27.gram_ref = f32[8,16,128]{2,1,0:T(8,128)S(1)} all-to-all(f32[8,16,128]{2,1,0:T(8,128)S(1)} %get-tuple-element.4), channel_id=1, replica_groups=mesh['far'=8,'near'=2,'x'=4,'y'=4,'core'=2] {'y','core'}, dimensions={0} | all-to-all | bytes 131072 | tf_op jit(solution)/shard_map/all_to_all | solution.py:238
  67.8 14.1 %all_to_all.28 = f32[8,8,128]{2,1,0:T(8,128)S(1)} all-to-all(f32[8,8,128]{2,1,0:T(8,128)S(1)} %broadcast_in_dim.4), channel_id=1, replica_groups=mesh['far'=8,'near'=2,'x'=4,'y'=4,'core'=2] {'far'}, dimensions={0} | all-to-all | bytes 65536 | tf_op jit(solution)/shard_map/all_to_all | solution.py:21
  82.0 0.7 broadcast_in_dim.5
  82.7 3.4 %all-to-all-start.4 = ((f32[8,8,8,128]{3,2,1,0:T(8,128)}), f32[8,8,8,128]{3,2,1,0:T(8,128)S(1)}, u32[]{:S(2)}, u32[]{:S(2)}) async-start(f32[8,8,8,128]{3,2,1,0:T(8,128)} %broadcast_in_dim.5), calls=%async_computation.4 | async-start | bytes 524288 | tf_op jit(solution)/shard_map/all_to_all | solution.py:21
  86.1 3.0 %shard_map.53.back_ref = f32[64,32]{1,0:T(8,128)S(1)} custom-call(f32[8,16,128]{2,1,0:T(8,128)S(1)} %all_to_all.27.gram_ref, f32[64,32]{1,0:T(8,128)S(1)} %get-tuple-element.5.left_ref), custom_call_target="tpu_custom_call" | custom-call | flops 131072 | bytes 65536 | tf_op jit(solution)/shard_map/pallas_call | solution.py:160
  89.1 3.0 %all-to-all-done.4 = f32[8,8,8,128]{3,2,1,0:T(8,128)S(1)} async-done(((f32[8,8,8,128]{3,2,1,0:T(8,128)}), f32[8,8,8,128]{3,2,1,0:T(8,128)S(1)}, u32[]{:S(2)}, u32[]{:S(2)}) %all-to-all-start.4) | async-done | bytes 262176 | tf_op jit(solution)/shard_map/all_to_all | solution.py:21
  92.1 4.9 %all-gather = f32[16,8,8,128]{3,2,1,0:T(8,128)S(1)} all-gather(f32[8,8,8,128]{3,2,1,0:T(8,128)S(1)} %all-to-all-done.4), channel_id=2, replica_groups=mesh['far'=8,'near'=2,'x'=4,'y'=4,'core'=2] {'core'}, dimensions={0}, use_global_device_ids=true | all-gather | bytes 786432 | tf_op jit(solution)/shard_map/all_gather | solution.py:240
  97.0 1.9 %shard_map.54 = (f32[64,4096]{1,0:T(8,128)}, f32[1,64,4096]{2,1,0:T(8,128)}) custom-call(f32[64,32]{1,0:T(8,128)S(1)} %shard_map.53.back_ref, f32[2,8,8,8,128]{4,3,2,1,0:T(8,128)S(1)} %bitcast.4, f32[8,272,128]{2,1,0:T(8,128)S(1)} %shard_map.50.sent_ref), custom_call_target="tpu_custom_call" | custom-call | tf_op jit(solution)/shard_map/pallas_call | solution.py:210
  (2 shorter events, 0.0 us)
Async XLA Ops:
  0.6 1.7 %copy-start = (f32[4096,32]{0,1:T(8,128)S(1)}, f32[4096,32]{0,1:T(8,128)}, u32[]{:S(2)}) copy-start(f32[4096,32]{0,1:T(8,128)} %param.5) | copy-start | bytes 1572868
  82.7 9.4 %all-to-all-start.4 = ((f32[8,8,8,128]{3,2,1,0:T(8,128)}), f32[8,8,8,128]{3,2,1,0:T(8,128)S(1)}, u32[]{:S(2)}, u32[]{:S(2)}) async-start(f32[8,8,8,128]{3,2,1,0:T(8,128)} %broadcast_in_dim.5), calls=%async_computation.4 | async-start | bytes 524288 | tf_op jit(solution)/shard_map/all_to_all | solution.py:21

commit v7 on v5

--- a/solution.py
+++ b/solution.py
@@ -231,7 +231,9 @@
     got, left_sum = middle(got, rows, rank, lax.axis_size(TENSOR))
     got = lax.all_to_all(got, TENSOR, 0, 0)
     back = solve(got, left_sum, lax.axis_size(DP))
-    whole = copies(copies(got[:, : rank // 2].sum(0), "far"), CLOSE)
+    mine = copies(got[:, : rank // 2].sum(0), "far")
+    mine, back = lax.optimization_barrier((mine, back))
+    whole = copies(mine, CLOSE)
     averaged, new_error = last(back, whole, sent)
     return (averaged, new_error)
 

time: 97.1 us -> 97.3 us (level)
  waiting for transfers between devices: 4.03 us -> 9.13 us
  blocking collectives: 78.4 us -> 74 us
    all_to_all x1, waiting for transfers between devices: 4.03 us -> 9.13 us  [copies(): lax.all_to_all(jnp.broadcast_to(block[None], (count,) + block.shape), axi...]
    all_to_all x1, blocking collectives: 14.5 us -> 10 us  [copies(): lax.all_to_all(jnp.broadcast_to(block[None], (count,) + block.shape), axi...]
where the time goes in v7:
time: 97.3 us; the launch traced here: 96 us
  blocking collectives  74 us (76%)
  waiting for transfers between devices  9.13 us (9%)
  Pallas kernels  6.52 us (7%)
  starting transfers between devices  3.35 us (3%)
  other arithmetic  1.72 us (2%)
    all_to_all x1, blocking collectives, shards(): lax.all_to_all(halve(got, rows, rows * rank // LANES, far), 'far', 0, 0)  31.2 us
    all_to_all x1, blocking collectives, shards(): got = lax.all_to_all(sent, CLOSE, 0, 0)  19.1 us
    all_to_all x1, blocking collectives, shards(): got = lax.all_to_all(got, TENSOR, 0, 0)  13.7 us
    all_to_all x1, blocking collectives, copies(): lax.all_to_all(jnp.broadcast_to(block[None], (count,) + block.shape), axi...  10 us
    all_to_all x1, waiting for transfers between devices, copies(): lax.all_to_all(jnp.broadcast_to(block[None], (count,) + block.shape), axi...  9.13 us
    all_to_all x1, starting transfers between devices, copies(): lax.all_to_all(jnp.broadcast_to(block[None], (count,) + block.shape), axi...  3.35 us
    pallas_call x1, Pallas kernels, solve(): pl.pallas_call(functools.partial(solve_kernel, replicas=float(replicas)),...  3.03 us
  transfers between devices with their start and end apart: 1, of which 1 were waited for; matrix products, arithmetic and copies ran while one was open for 0% of the time, Pallas kernels for 3%

profile of v7, /device:TPU:1, one launch (start us, length us, event | category | flops | bytes accessed | tf_op | source)
XLA Modules:
  0.0 96.0 jit_solution(17588614004101746584)
XLA Ops:
  0.6 0.0 copy-start
  0.6 1.7 %add_bitcast_fusion.corrected_ref = f32[64,4096]{1,0:T(8,128)S(1)} fusion(f32[1,64,4096]{2,1,0:T(8,128)} %param.3, f32[1,64,4096]{2,1,0:T(8,128)} %param.4), kind=kLoop, calls=%fused_computation | loop fusion | flops 262144 | bytes 3145728 | tf_op jit(solution)/shard_map/add | solution.py:226
  2.3 0.0 copy-done
  2.4 1.0 %shard_map.50.sent_ref = f32[8,272,128]{2,1,0:T(8,128)S(1)} custom-call(f32[64,4096]{1,0:T(8,128)S(1)} %add_bitcast_fusion.corrected_ref, f32[32,4096]{1,0:T(8,128)S(1)} %bitcast.3), custom_call_target="tpu_custom_call" | custom-call | tf_op jit(solution)/shard_map/pallas_call | solution.py:51
  3.4 19.1 %all_to_all.25.got_ref = f32[8,272,128]{2,1,0:T(8,128)S(1)} all-to-all(f32[8,272,128]{2,1,0:T(8,128)S(1)} %shard_map.50.sent_ref), channel_id=1, replica_groups=mesh['far'=8,'near'=2,'x'=4,'y'=4,'core'=2] {'near','x'}, dimensions={0} | all-to-all | bytes 2228224 | tf_op jit(solution)/shard_map/all_to_all | solution.py:228
  22.5 0.1 shard_map.51
  22.6 31.2 %all_to_all.26.got_ref = f32[8,48,128]{2,1,0:T(8,128)S(1)} all-to-all(f32[8,48,128]{2,1,0:T(8,128)S(1)} %shard_map.51), channel_id=1, replica_groups=mesh['far'=8,'near'=2,'x'=4,'y'=4,'core'=2] {'far'}, dimensions={0} | all-to-all | bytes 393216 | tf_op jit(solution)/shard_map/all_to_all | solution.py:229
  53.8 0.5 shard_map.52
  54.3 13.7 %all_to_all.27.gram_ref = f32[8,24,128]{2,1,0:T(8,128)S(1)} all-to-all(f32[8,24,128]{2,1,0:T(8,128)S(1)} %get-tuple-element.6), channel_id=1, replica_groups=mesh['far'=8,'near'=2,'x'=4,'y'=4,'core'=2] {'y','core'}, dimensions={0} | all-to-all | bytes 196608 | tf_op jit(solution)/shard_map/all_to_all | solution.py:232
  67.9 0.6 broadcast_in_dim.4
  68.6 3.4 %all-to-all-start.3 = ((f32[8,16,128]{2,1,0:T(8,128)}), f32[8,16,128]{2,1,0:T(8,128)S(1)}, u32[]{:S(2)}, u32[]{:S(2)}) async-start(f32[8,16,128]{2,1,0:T(8,128)} %broadcast_in_dim.4), calls=%async_computation.3 | async-start | bytes 131072 | tf_op jit(solution)/shard_map/all_to_all | solution.py:21
  71.9 3.0 %shard_map.53.back_ref = f32[64,32]{1,0:T(8,128)S(1)} custom-call(f32[8,24,128]{2,1,0:T(8,128)S(1)} %all_to_all.27.gram_ref, f32[64,32]{1,0:T(8,128)S(1)} %get-tuple-element.7.left_ref), custom_call_target="tpu_custom_call" | custom-call | flops 131072 | bytes 65536 | tf_op jit(solution)/shard_map/pallas_call | solution.py:158
  75.0 9.1 %all-to-all-done.3 = f32[8,16,128]{2,1,0:T(8,128)S(1)} async-done(((f32[8,16,128]{2,1,0:T(8,128)}), f32[8,16,128]{2,1,0:T(8,128)S(1)}, u32[]{:S(2)}, u32[]{:S(2)}) %all-to-all-start.3) | async-done | bytes 65568 | tf_op jit(solution)/shard_map/all_to_all | solution.py:21
  84.2 10.0 %all_to_all.28.whole_ref = f32[8,8,16,128]{3,2,1,0:T(8,128)S(1)} all-to-all(f32[8,8,16,128]{3,2,1,0:T(8,128)S(1)} %broadcast_in_dim.5), channel_id=1, replica_groups=mesh['far'=8,'near'=2,'x'=4,'y'=4,'core'=2] {'near','x'}, dimensions={0} | all-to-all | bytes 1048576 | tf_op jit(solution)/shard_map/all_to_all | solution.py:21
  94.2 1.9 %shard_map.54 = (f32[64,4096]{1,0:T(8,128)}, f32[1,64,4096]{2,1,0:T(8,128)}) custom-call(f32[64,32]{1,0:T(8,128)S(1)} %shard_map.53.back_ref, f32[8,8,16,128]{3,2,1,0:T(8,128)S(1)} %all_to_all.28.whole_ref, f32[8,272,128]{2,1,0:T(8,128)S(1)} %shard_map.50.sent_ref), custom_call_target="tpu_custom_call" | custom-call | tf_op jit(solution)/shard_map/pallas_call | solution.py:204
  (2 shorter events, 0.0 us)
Async XLA Ops:
  0.6 1.7 %copy-start = (f32[4096,32]{0,1:T(8,128)S(1)}, f32[4096,32]{0,1:T(8,128)}, u32[]{:S(2)}) copy-start(f32[4096,32]{0,1:T(8,128)} %param.5) | copy-start | bytes 1572868
  68.6 15.5 %all-to-all-start.3 = ((f32[8,16,128]{2,1,0:T(8,128)}), f32[8,16,128]{2,1,0:T(8,128)S(1)}, u32[]{:S(2)}, u32[]{:S(2)}) async-start(f32[8,16,128]{2,1,0:T(8,128)} %broadcast_in_dim.4), calls=%async_computation.3 | async-start | bytes 131072 | tf_op jit(solution)/shard_map/all_to_all | solution.py:21
